TPU v7x, 32 devices: a whole 2x2x4 slice. The times are simulated.
32 devices in a mesh: ctx: 8 (over z, x), head: 4 (over y, core).
Axes of the slice: x: 2, y: 2, z: 4, core: 2. Of those that a mesh axis runs over, the one named last changes fastest.
Arguments:
- inputs: bfloat16 [1536, 2048], P('ctx'), may hold values from -6 to 6
- projection: bfloat16 [3, 2048, 1024], P(None, None, 'head'), may hold values from -0.125 to 0.125
- conv_weight: float32 [3, 4, 1024], P(None, None, 'head'), may hold values from -3 to 3
- gate_code: int32 [8, 1536], P('head', 'ctx'), may hold values from 0 to 1023
- beta_code: int32 [8, 1536], P('head', 'ctx'), may hold values from 0 to 1023
- grad_out: bfloat16 [1536, 1024], P('ctx', 'head'), may hold values from -6 to 6
Outputs:
- input_grad: bfloat16 [1536, 2048], P(('ctx', 'head'))
- kernel_grad: float32 [3, 4, 1024], P(None, None, 'head')
All inputs are finite; a program needn't handle non-finite values.
Results may differ from a plain program's by a relative error of at most 0.0068.
The roundings to bfloat16 on the way count: a program that leaves them out, or rounds other values in their place, can miss the bound.
Values may be sent and summed in bfloat16 or wider, within the bound.
A program may use at most 64 MiB of HBM per device.

v0:
```python
import jax
import jax.numpy as jnp
from jax import lax
from jax.sharding import PartitionSpec as P

DK = 128
KW = 4
GROUP = 64


HIGHEST_PRECISION = lax.Precision.HIGHEST


def from_behind(block, axis, distance):
    devices = range(lax.axis_size(axis))
    route = [(i - distance, i) for i in devices if i - distance in devices]
    return lax.ppermute(block, axis, route)


def carried_in(part, axis, combine, identity, reverse):
    count = lax.axis_size(axis)
    place = lax.axis_index(axis)
    ahead = count - 1 - place if reverse else place
    gathered = jax.tree.map(lambda a: lax.all_gather(a, axis), part)
    state = jax.tree.map(lambda a, e: jnp.zeros_like(a) + jnp.asarray(e, a.dtype), part, identity)

    def one(step, state):
        source = count - 1 - step if reverse else step
        return combine(
            state, jax.tree.map(lambda a: lax.dynamic_index_in_dim(a, source, 0, False), gathered)
        )

    return lax.fori_loop(0, ahead, one, state)


def normalize(matrix):
    return matrix * lax.rsqrt(jnp.sum(matrix * matrix, -1, keepdims=True) + 1e-06)


def features(extended, weights):
    length = extended.shape[1] - (KW - 1)
    convolved = weights[:, 0:1, :] * extended[:, 0:length, :]
    for offset in range(1, KW):
        convolved = (
            convolved
            + weights[:, offset : offset + 1, :] * extended[:, offset : offset + length, :]
        )
    activated = jax.nn.silu(convolved)
    head_count = activated.shape[2] // DK
    activated = activated.reshape(3, length, head_count, DK).transpose(0, 2, 1, 3)
    queries = normalize(activated[0]) * DK ** (-0.5)
    norm_keys = normalize(activated[1])
    return (queries, norm_keys, activated[2])


def block_step(carried, pieces):
    queries, norm_keys, value_rows, log_gate, beta_rate = pieces
    cumulative = jnp.cumsum(log_gate, axis=-1)
    decay_now = jnp.exp(cumulative)
    between = cumulative[:, :, None] - cumulative[:, None, :]
    position = jnp.arange(log_gate.shape[-1])
    strict = position[:, None] > position[None, :]
    inclusive = position[:, None] >= position[None, :]
    key_gram = jnp.einsum("htd,hsd->hts", norm_keys, norm_keys, precision=HIGHEST_PRECISION)
    lower_part = jnp.where(strict, jnp.exp(between), 0.0) * key_gram * beta_rate[:, :, None]
    recalled = jnp.einsum("htd,hvd->htv", norm_keys, carried, precision=HIGHEST_PRECISION)
    target = beta_rate[:, :, None] * (value_rows - decay_now[:, :, None] * recalled)
    pseudo = jax.scipy.linalg.solve_triangular(lower_part, target, lower=True, unit_diagonal=True)
    scores = jnp.einsum(
        "htd,hsd->hts", queries, norm_keys, precision=HIGHEST_PRECISION
    ) * jnp.where(inclusive, jnp.exp(between), 0.0)
    outputs = decay_now[:, :, None] * jnp.einsum(
        "htd,hvd->htv", queries, carried, precision=HIGHEST_PRECISION
    )
    outputs = outputs + jnp.einsum("hts,hsv->htv", scores, pseudo, precision=HIGHEST_PRECISION)
    group_total = cumulative[:, -1]
    remaining = jnp.exp(group_total[:, None] - cumulative)
    new_state = jnp.exp(group_total)[:, None, None] * carried
    new_state = new_state + jnp.einsum(
        "hsv,hsd->hvd", pseudo, remaining[:, :, None] * norm_keys, precision=HIGHEST_PRECISION
    )
    return (new_state, outputs)


def run_blocks(queries, norm_keys, value_rows, log_gate, beta_rate, carried):
    head_count = queries.shape[0]
    length = queries.shape[1]
    blocks = length // GROUP

    def to_blocks(tensor):
        return jnp.moveaxis(
            tensor.reshape((tensor.shape[0], blocks, GROUP) + tensor.shape[2:]), 1, 0
        )

    final_state, outputs = lax.scan(
        block_step,
        carried,
        (
            to_blocks(queries),
            to_blocks(norm_keys),
            to_blocks(value_rows),
            to_blocks(log_gate),
            to_blocks(beta_rate),
        ),
    )
    outputs = jnp.moveaxis(outputs, 0, 1).reshape(head_count, length, DK)
    return (outputs, final_state)


def chain_product(left_side, right_side):
    return jnp.einsum("hij,hjk->hik", left_side, right_side, precision=HIGHEST_PRECISION)


def compose(earlier, later):
    return (chain_product(earlier[0], later[0]), chain_product(earlier[1], later[0]) + later[1])


def on_device(inputs, projection, conv_weight, gate_code, beta_code, grad_out):
    length = inputs.shape[0]
    head_count = gate_code.shape[0]
    projected = jnp.stack(
        [
            jnp.dot(inputs, projection[member], preferred_element_type=jnp.float32)
            for member in range(3)
        ]
    ).astype(jnp.bfloat16)
    tail_rows = projected[:, length - (KW - 1) :, :]
    earlier_rows = from_behind(tail_rows, "ctx", 1)
    extended = jnp.concatenate([earlier_rows, projected], 1).astype(jnp.float32)
    log_gate = jnp.log(1.0 - 0.001 * gate_code.astype(jnp.float32) / 1023.0)
    beta_rate = beta_code.astype(jnp.float32) / 1023.0
    (queries, norm_keys, value_rows), feature_pull = jax.vjp(features, extended, conv_weight)
    identity = jnp.broadcast_to(jnp.eye(DK, dtype=jnp.float32), (head_count, DK, DK))
    zero_state = jnp.zeros((head_count, DK, DK), jnp.float32)
    paired = run_blocks(
        jnp.concatenate([queries, queries], 0),
        jnp.concatenate([norm_keys, norm_keys], 0),
        jnp.concatenate([value_rows, jnp.zeros_like(value_rows)], 0),
        jnp.concatenate([log_gate, log_gate], 0),
        jnp.concatenate([beta_rate, beta_rate], 0),
        jnp.concatenate([zero_state, identity], 0),
    )[1]
    local_state = paired[:head_count]
    transition = paired[head_count:]
    entering = carried_in((transition, local_state), "ctx", compose, (identity, zero_state), False)[
        1
    ]

    def core(query_part, key_part, value_part, start_state):
        return run_blocks(query_part, key_part, value_part, log_gate, beta_rate, start_state)

    (outputs, leaving), core_pull = jax.vjp(core, queries, norm_keys, value_rows, entering)
    cotangent = grad_out.astype(jnp.float32).reshape(length, head_count, DK).transpose(1, 0, 2)
    direct_grads = core_pull((cotangent, zero_state))
    local_adjoint = direct_grads[3]
    flipped = jnp.swapaxes(transition, 1, 2)
    arriving = carried_in((flipped, local_adjoint), "ctx", compose, (identity, zero_state), True)[1]
    carried_grads = core_pull((jnp.zeros_like(outputs), arriving))
    feature_grads = tuple((direct_grads[member] + carried_grads[member] for member in range(3)))
    extended_grad, weight_grad = feature_pull(feature_grads)
    spill_rows = extended_grad[:, : KW - 1, :]
    returned = from_behind(spill_rows, "ctx", -1)
    raw_grad = extended_grad[:, KW - 1 :, :]
    raw_grad = raw_grad.at[:, length - (KW - 1) :, :].add(returned)
    rounded = raw_grad.astype(jnp.bfloat16)
    input_grad = lax.psum_scatter(
        jnp.einsum("mtc,mdc->td", rounded, projection, preferred_element_type=jnp.float32),
        "head",
        scatter_dimension=0,
        tiled=True,
    ).astype(jnp.bfloat16)
    kernel_grad = lax.psum(weight_grad, "ctx")
    return (input_grad, kernel_grad)


def solution(mesh):
    return jax.shard_map(
        on_device,
        mesh=mesh,
        in_specs=(
            P("ctx", None),
            P(None, None, "head"),
            P(None, None, "head"),
            P("head", "ctx"),
            P("head", "ctx"),
            P("ctx", "head"),
        ),
        out_specs=(P(("ctx", "head"), None), P(None, None, "head")),
        check_vma=False,
    )
```

profile of v0, /device:TPU:0, one launch (start us, length us, event | category | flops | bytes accessed | tf_op | source)
XLA Modules:
  0.0 481.3 jit_solution(11471538402848206259)
XLA Ops:
  7.3 1.0 copy-done
  8.3 1.6 fusion.198
  9.9 1.6 fusion.199
  11.5 1.6 fusion.200
  13.1 4.8 %collective-permute-start = (bf16[3,3,256]{2,1,0:T(4,128)(2,1)S(1)}, bf16[3,3,256]{2,1,0:T(4,128)(2,1)S(1)}, u32[]{:S(2)}, u32[]{:S(2)}) collective-permute-start(bf16[3,3,256]{2,1,0:T(4,128)(2,1)S(1)} %pad_maximum_fusion), channel_id=1, source_target_pairs={{0,4},{4,8},{8,12},{12,16},{16,20},{20,24},{24,28},{1,5},{5,9},{9,... | collective-permute-start | bytes 13832 | tf_op jit(solution)/shard_map/ppermute | solution.py:17
  19.4 1.2 multiply_bitcast_fusion
  23.9 71.5 %while.120 = (s32[]{:T(128)}, f32[4,128,128]{2,1,0:T(8,128)S(1)}, f32[3,4,64]{2,0,1:T(4,128)S(1)}, f32[3,4,64,128]{3,2,0,1:T(8,128)S(1)}, f32[3,4,64]{2,0,1:T(4,...) while((s32[]{:T(128)}, f32[4,128,128]{2,1,0:T(8,128)S(1)}, f32[3,4,64]{2,0,1:T(4,128)S(1)}, ...), condition=%wide.region_3.4_spmd, body=%wide.region_1.0_spmd.sunk | while | flops 151388224 | bytes 2063541 | solution.py:95
  26.2 20.4 %custom-call.38 = f32[4,1,64,64]{2,3,1,0:T(8,128)S(1)} custom-call(f32[4,1,64,64]{3,2,1,0:T(8,128)} %fusion.352), custom_call_target="InvertDiagBlocksLowerTriangular" | custom-call | tf_op jit(solution)/shard_map/while/body/eval_jaxpr/jit(_solve_triangular)/vmap()/triangular_solve | solution.py:68
  50.0 20.4 %custom-call.38 = f32[4,1,64,64]{2,3,1,0:T(8,128)S(1)} custom-call(f32[4,1,64,64]{3,2,1,0:T(8,128)} %fusion.352), custom_call_target="InvertDiagBlocksLowerTriangular" | custom-call | tf_op jit(solution)/shard_map/while/body/eval_jaxpr/jit(_solve_triangular)/vmap()/triangular_solve | solution.py:68
  73.9 20.4 %custom-call.38 = f32[4,1,64,64]{2,3,1,0:T(8,128)S(1)} custom-call(f32[4,1,64,64]{3,2,1,0:T(8,128)} %fusion.352), custom_call_target="InvertDiagBlocksLowerTriangular" | custom-call | tf_op jit(solution)/shard_map/while/body/eval_jaxpr/jit(_solve_triangular)/vmap()/triangular_solve | solution.py:68
  101.4 37.1 %all-gather.9.cloned.1.call-done = f32[16,128,128]{2,1,0:T(8,128)} async-done(((f32[2,128,128]{2,1,0:T(8,128)}), f32[16,128,128]{2,1,0:T(8,128)}) %all-gather.9.cloned.1.call-update) | async-done | bytes 1048592 | tf_op jit(solution)/shard_map/all_gather | solution.py:24
  138.5 41.6 %all-gather.11.cloned.1.call-done = f32[16,128,128]{2,1,0:T(8,128)} async-done(((f32[2,128,128]{2,1,0:T(8,128)}), f32[16,128,128]{2,1,0:T(8,128)}) %all-gather.11.cloned.1.call-update) | async-done | bytes 1048592 | tf_op jit(solution)/shard_map/all_gather | solution.py:24
  180.3 49.0 %while.124 = (s32[]{:T(128)}, f32[2,128,128]{2,1,0:T(8,128)S(1)}, f32[3,2,64,64]{3,2,1,0:T(8,128)}, f32[3,2,64,1]{2,1,3,0:T(2,128)S(1)}, f32[3,2,128,128]{3,2,1,...) while((s32[]{:T(128)}, f32[2,128,128]{2,1,0:T(8,128)S(1)}, ...), condition=%wide.region_9.10_spmd.clone.clone, body=%wide.region_7.9_spmd.clone.clone.sunk | while | flops 88346816 | bytes 2198809 | solution.py:95
  182.9 9.9 %custom-call.40 = f32[2,1,64,64]{2,3,1,0:T(8,128)S(1)} custom-call(f32[2,1,64,64]{3,2,1,0:T(8,128)S(1)} %add_bitcast_fusion.4), custom_call_target="InvertDiagBlocksLowerTriangular" | custom-call | tf_op jit(solution)/shard_map/jvp()/while/body/eval_jaxpr/jit(_solve_triangular)/vmap()/triangular_solve | solution.py:68
  199.3 9.8 %custom-call.40 = f32[2,1,64,64]{2,3,1,0:T(8,128)S(1)} custom-call(f32[2,1,64,64]{3,2,1,0:T(8,128)S(1)} %add_bitcast_fusion.4), custom_call_target="InvertDiagBlocksLowerTriangular" | custom-call | tf_op jit(solution)/shard_map/jvp()/while/body/eval_jaxpr/jit(_solve_triangular)/vmap()/triangular_solve | solution.py:68
  215.6 9.8 %custom-call.40 = f32[2,1,64,64]{2,3,1,0:T(8,128)S(1)} custom-call(f32[2,1,64,64]{3,2,1,0:T(8,128)S(1)} %add_bitcast_fusion.4), custom_call_target="InvertDiagBlocksLowerTriangular" | custom-call | tf_op jit(solution)/shard_map/jvp()/while/body/eval_jaxpr/jit(_solve_triangular)/vmap()/triangular_solve | solution.py:68
  230.7 58.5 %while.125 = (s32[]{:T(128)}, f32[2,128,128]{2,1,0:T(8,128)S(1)}, f32[3,2,64,128]{3,2,0,1:T(8,128)S(1)}, f32[3,2,64,128]{3,2,0,1:T(8,128)}, f32[3,2,64,128]{3,2,...) while((s32[]{:T(128)}, f32[2,128,128]{2,1,0:T(8,128)S(1)}, ...), condition=%wide.region_11.13_spmd.clone, body=%wide.region_10.12_spmd.clone.sunk | while | flops 258445376 | bytes 4060456 | solution.py:95
  230.7 1.2 fusion.431
  231.9 1.0 convolution_add_fusion.41
  233.0 9.8 %custom-call.41 = f32[2,1,64,64]{2,3,1,0:T(8,128)S(1)} custom-call(f32[2,1,64,64]{3,2,1,0:T(8,128)S(1)} %fusion.432), custom_call_target="InvertDiagBlocksLowerTriangular" | custom-call | tf_op jit(solution)/shard_map/transpose(jvp())/while/body/eval_jaxpr/jit(_solve_triangular)/vmap()/triangular_solve | solution.py:68
  243.9 1.1 convolution_multiply_fusion.17
  245.9 1.0 fusion.437
  250.1 1.2 fusion.431
  251.3 1.0 convolution_add_fusion.41
  252.5 9.8 %custom-call.41 = f32[2,1,64,64]{2,3,1,0:T(8,128)S(1)} custom-call(f32[2,1,64,64]{3,2,1,0:T(8,128)S(1)} %fusion.432), custom_call_target="InvertDiagBlocksLowerTriangular" | custom-call | tf_op jit(solution)/shard_map/transpose(jvp())/while/body/eval_jaxpr/jit(_solve_triangular)/vmap()/triangular_solve | solution.py:68
  263.4 1.1 convolution_multiply_fusion.17
  265.4 1.0 fusion.437
  269.7 1.2 fusion.431
  270.9 1.0 convolution_add_fusion.41
  272.0 9.8 %custom-call.41 = f32[2,1,64,64]{2,3,1,0:T(8,128)S(1)} custom-call(f32[2,1,64,64]{3,2,1,0:T(8,128)S(1)} %fusion.432), custom_call_target="InvertDiagBlocksLowerTriangular" | custom-call | tf_op jit(solution)/shard_map/transpose(jvp())/while/body/eval_jaxpr/jit(_solve_triangular)/vmap()/triangular_solve | solution.py:68
  283.0 1.1 convolution_multiply_fusion.17
  284.9 1.0 fusion.437
  289.9 55.6 %all-gather.15.cloned.1.call-done = f32[16,128,128]{2,1,0:T(8,128)} async-done(((f32[2,128,128]{2,1,0:T(8,128)}), f32[16,128,128]{2,1,0:T(8,128)}) %all-gather.15.cloned.1.call-update) | async-done | bytes 1048592 | tf_op jit(solution)/shard_map/all_gather | solution.py:24
  345.5 16.8 %while.122 = (s32[]{:T(128)}, f32[2,128,128]{1,2,0:T(8,128)S(1)}, s32[]{:T(128)}, f32[8,2,128,128]{3,2,1,0:T(8,128)}, f32[8,2,128,128]{3,2,1,0:T(8,128)}, /*index=5*/s32[]{:T(128)}, s32[]{:T(128)}, s32[]{:T(128)}, s32[]{:T(128)}) while((s32[]{:T(128)}, f32[2,128,128]{1,2,0:T(8,128)S(1)}, s32[]{:T(128)}, f32[8,2,128,128]{3,2,1,0:T(8,128)}, ...), condition=%wide.region_13.15_spmd, body=%wide.region_12.14_spmd.sunk | while | flops 50364420 | bytes 1310867 | solution.py:33
  346.6 1.3 fusion.359
  349.0 1.3 fusion.359
  351.3 1.3 fusion.359
  353.7 1.3 fusion.359
  356.1 1.3 fusion.359
  358.5 1.3 fusion.359
  360.8 1.3 fusion.359
  364.5 60.3 %while.123 = (s32[]{:T(128)}, f32[2,128,128]{2,1,0:T(8,128)S(1)}, f32[3,2,64,128]{3,2,0,1:T(8,128)}, f32[3,2,64,128]{3,2,0,1:T(8,128)}, f32[3,2,64,128]{3,2,0,1:...) while((s32[]{:T(128)}, f32[2,128,128]{2,1,0:T(8,128)S(1)}, ...), condition=%wide.region_15.17_spmd.clone, body=%wide.region_14.16_spmd.clone.sunk | while | flops 258314432 | bytes 3794713 | solution.py:95
  364.6 1.3 fusion.388
  365.8 1.0 convolution_add_fusion.34
  367.0 9.8 %custom-call.39 = f32[2,1,64,64]{2,3,1,0:T(8,128)S(1)} custom-call(f32[2,1,64,64]{3,2,1,0:T(8,128)S(1)} %fusion.389), custom_call_target="InvertDiagBlocksLowerTriangular" | custom-call | tf_op jit(solution)/shard_map/transpose(jvp())/while/body/eval_jaxpr/jit(_solve_triangular)/vmap()/triangular_solve | solution.py:68
  377.9 1.1 convolution_multiply_fusion.15
  379.8 1.0 fusion.394
  384.7 1.2 fusion.388
  385.9 1.0 convolution_add_fusion.34
  387.0 9.8 %custom-call.39 = f32[2,1,64,64]{2,3,1,0:T(8,128)S(1)} custom-call(f32[2,1,64,64]{3,2,1,0:T(8,128)S(1)} %fusion.389), custom_call_target="InvertDiagBlocksLowerTriangular" | custom-call | tf_op jit(solution)/shard_map/transpose(jvp())/while/body/eval_jaxpr/jit(_solve_triangular)/vmap()/triangular_solve | solution.py:68
  397.9 1.1 convolution_multiply_fusion.15
  399.9 1.0 fusion.394
  404.8 1.2 fusion.388
  407.1 9.8 %custom-call.39 = f32[2,1,64,64]{2,3,1,0:T(8,128)S(1)} custom-call(f32[2,1,64,64]{3,2,1,0:T(8,128)S(1)} %fusion.389), custom_call_target="InvertDiagBlocksLowerTriangular" | custom-call | tf_op jit(solution)/shard_map/transpose(jvp())/while/body/eval_jaxpr/jit(_solve_triangular)/vmap()/triangular_solve | solution.py:68
  418.1 1.1 convolution_multiply_fusion.15
  420.0 1.0 fusion.394
  424.9 1.1 broadcast_multiply_fusion.5
  426.0 1.0 add.271
  427.3 1.0 add.268
  429.4 1.3 collective-permute-start.1
  431.0 4.0 collective-permute-done.1
  435.2 4.2 convolution_bitcast_fusion.2
  439.5 33.0 %psum.7 = f32[3,4,256]{2,0,1:T(4,128)S(1)} all-reduce(f32[3,4,256]{2,0,1:T(4,128)S(1)} %pad_add_fusion.1), channel_id=1, replica_groups=mesh['ctx'=8,'head'=4] {'ctx'}, use_global_device_ids=true, to_apply=%region_23.25 | all-reduce | flops 3072 | bytes 24576 | tf_op jit(solution)/shard_map/psum | solution.py:172
  473.1 1.7 convert_element_type.25
  (336 shorter events, 87.7 us)
Async XLA Ops:
  7.2 1.1 copy-start
  7.2 10.8 %copy-start.11 = (f32[3,4,256]{2,1,0:T(4,128)S(1)}, f32[3,4,256]{2,1,0:T(4,128)}, u32[]{:S(2)}) copy-start(f32[3,4,256]{2,1,0:T(4,128)} %param.26) | copy-start | bytes 36868
  7.2 10.8 %copy-start.12 = (s32[2,192]{1,0:T(2,128)S(1)}, s32[2,192]{1,0:T(2,128)}, u32[]{:S(2)}) copy-start(s32[2,192]{1,0:T(2,128)} %param.27) | copy-start | bytes 4612
  7.2 10.9 %copy-start.13 = (s32[2,192]{1,0:T(2,128)S(1)}, s32[2,192]{1,0:T(2,128)}, u32[]{:S(2)}) copy-start(s32[2,192]{1,0:T(2,128)} %param.28) | copy-start | bytes 4612
  7.2 131.3 %all-gather.9.cloned.1.call-start = ((), (), s32[]{:S(2)}) async-start(), calls=%async_computation.2 | async-start | bytes 1179648 | tf_op jit(solution)/shard_map/all_gather | solution.py:24
  13.1 6.2 %collective-permute-start = (bf16[3,3,256]{2,1,0:T(4,128)(2,1)S(1)}, bf16[3,3,256]{2,1,0:T(4,128)(2,1)S(1)}, u32[]{:S(2)}, u32[]{:S(2)}) collective-permute-start(bf16[3,3,256]{2,1,0:T(4,128)(2,1)S(1)} %pad_maximum_fusion), channel_id=1, source_target_pairs={{0,4},{4,8},{8,12},{12,16},{16,20},{20,24},{24,28},{1,5},{5,9},{9,... | collective-permute-start | bytes 13832 | tf_op jit(solution)/shard_map/ppermute | solution.py:17
  20.6 0.9 copy-start.2
  22.2 0.6 copy-start.8
  22.2 0.6 copy-start.6
  96.2 84.0 %all-gather.11.cloned.1.call-start = ((), (), s32[]{:S(2)}) async-start(), calls=%async_computation.3 | async-start | bytes 1179648 | tf_op jit(solution)/shard_map/all_gather | solution.py:24
  96.9 193.0 %all-gather.13.cloned.1.call-start = ((), (), s32[]{:S(2)}) async-start(), calls=%async_computation.4 | async-start | bytes 1179648 | tf_op jit(solution)/shard_map/all_gather | solution.py:24
  101.3 244.2 %all-gather.15.cloned.1.call-start = ((), (), s32[]{:S(2)}) async-start(), calls=%async_computation.5 | async-start | bytes 1179648 | tf_op jit(solution)/shard_map/all_gather | solution.py:24
  289.2 0.6 copy-start.1
  289.2 56.3 %copy-start.5 = (f32[3,2,64,128]{3,2,0,1:T(8,128)}, f32[3,2,64,128]{3,2,0,1:T(8,128)S(1)}, u32[]{:S(2)}) copy-start(f32[3,2,64,128]{3,2,0,1:T(8,128)S(1)} %get-tuple-element.1352) | copy-start | bytes 589828
  289.8 183.2 %reduce-scatter.2.cloned.1.call-start = ((), (), s32[]{:S(2)}) async-start(), calls=%async_computation.1 | async-start | bytes 1966080 | tf_op jit(solution)/shard_map/reduce_scatter | solution.py:166
  364.5 62.5 %copy-start.3 = (f32[3,24,2,8,128]{4,3,1,2,0:T(8,128)S(1)}, f32[3,24,2,8,128]{4,3,1,2,0:T(8,128)}, u32[]{:S(2)}) copy-start(f32[3,24,2,8,128]{4,3,1,2,0:T(8,128)} %copy-done.2) | copy-start | bytes 1769476
  364.5 62.8 %copy-start.10 = (f32[2,192]{1,0:T(2,128)S(1)}, f32[2,192]{1,0:T(2,128)}, u32[]{:S(2)}) copy-start(f32[2,192]{1,0:T(2,128)} %get-tuple-element.1850) | copy-start | bytes 4612
  364.5 62.8 %copy-start.9 = (f32[2,192]{1,0:T(2,128)S(1)}, f32[2,192]{1,0:T(2,128)}, u32[]{:S(2)}) copy-start(f32[2,192]{1,0:T(2,128)} %copy-done.8) | copy-start | bytes 4612
  364.5 63.9 %copy-start.7 = (f32[2,192]{1,0:T(2,128)S(1)}, f32[2,192]{1,0:T(2,128)}, u32[]{:S(2)}) copy-start(f32[2,192]{1,0:T(2,128)} %copy-done.6) | copy-start | bytes 4612
  424.9 3.8 copy-start.4
  429.4 5.6 %collective-permute-start.1 = (f32[3,3,256]{2,1,0:T(4,128)S(1)}, f32[3,3,256]{2,1,0:T(4,128)S(1)}, u32[]{:S(2)}, u32[]{:S(2)}) collective-permute-start(f32[3,3,256]{2,1,0:T(4,128)S(1)} %pad_add_fusion.2), channel_id=1, source_target_pairs={{4,0},{8,4},{12,8},{16,12},{20,16},{24,20},{28,24},{5,1},{9,5},{13... | collective-permute-start | bytes 27656 | tf_op jit(solution)/shard_map/ppermute | solution.py:17
Sparse Core Ops, SparseCore 0:
  96.3 42.1 all-gather.8
  141.2 38.8 all-gather.10
  182.3 39.9 all-gather.12
  290.0 55.4 all-gather.14
  439.6 25.3 reduce-scatter.1
where the time goes:
time: 484 us; the launch traced here: 481 us
  other arithmetic  167 us (35%)
  waiting for transfers between devices  140 us (29%)
  matrix products  85.7 us (18%)
  local copies, waits for them, and re-layouts  33.2 us (7%)
  blocking collectives  33 us (7%)
  between operations  14.3 us (3%)
  starting transfers between devices  6.33 us (1%)
    another operation x45, other arithmetic, block_step(): jax.scipy.linalg.solve_triangular(lower_part, target, lower=True, unit_di...  151 us
    all_gather x4, waiting for transfers between devices, carried_in(): gathered = jax.tree.map(lambda a: lax.all_gather(a, axis), part)  134 us
    psum x1, blocking collectives, on_device(): kernel_grad = lax.psum(weight_grad, 'ctx')  33 us
    another operation x18, matrix products, block_step(): jax.scipy.linalg.solve_triangular(lower_part, target, lower=True, unit_di...  13.3 us
    dot_general x12, matrix products, block_step(): jnp.einsum('hts,hsv->htv', scores, pseudo, precision=HIGHEST_PRECISION)  12.7 us
    dot_general x18, matrix products, block_step(): jnp.einsum('hsv,hsd->hvd', pseudo, remaining[:, :, None] * norm_keys, pre...  12.2 us
    dot_general x18, matrix products, block_step(): jnp.einsum('htd,hsd->hts', norm_keys, norm_keys, precision=HIGHEST_PRECIS...  10.5 us
  transfers between devices with their start and end apart: 7, of which 5 were waited for; matrix products, arithmetic and copies ran while one was open for 24% of the time, Pallas kernels for 0%

commit v1 on v0

v1 whole, which is shorter than its diff:
```python
import functools

import jax
import jax.numpy as jnp
from jax import lax
from jax.experimental import pallas as pl
from jax.experimental.pallas import tpu as pltpu
from jax.sharding import PartitionSpec as P

DK = 128
KW = 4
HALO = 16
F32 = jnp.float32
BF16 = jnp.bfloat16
VMEM = pl.BlockSpec(memory_space=pltpu.VMEM)


def contract(a, b, dims, precise):
    if precise:
        return lax.dot_general(
            a, b, (dims, ((), ())), precision=lax.Precision.HIGHEST, preferred_element_type=F32
        )
    return lax.dot_general(
        a.astype(BF16), b.astype(BF16), (dims, ((), ())), preferred_element_type=F32
    )


def nn(a, b, precise=False):
    return contract(a, b, ((1,), (0,)), precise)


def nt(a, b, precise=False):
    return contract(a, b, ((1,), (1,)), precise)


def tn(a, b, precise=False):
    return contract(a, b, ((0,), (0,)), precise)


def unit_inverses(lowers, eye, distance):
    count = eye.shape[0]
    inverses = [eye - jnp.where(distance == 1, low, 0.0) for low in lowers]
    size = 2
    while size < count:
        mask = (distance >= size) & (distance < 2 * size)
        inner = [nn(inv, jnp.where(mask, low, 0.0)) for inv, low in zip(inverses, lowers)]
        inverses = [inv - nn(mid, inv) for inv, mid in zip(inverses, inner)]
        size *= 2
    left = [eye - inv - nn(low, inv, True) for inv, low in zip(inverses, lowers)]
    return [inv + nn(inv, rest) for inv, rest in zip(inverses, left)]


def local_part(tail, x_ref, w_ref, cw_ref, gate_ref, beta_ref, g_ref, ext, heads):
    count = x_ref.shape[0]
    for m in range(3):
        weights = w_ref[m]
        ext[m, HALO:, :] = nn(x_ref[...], weights).astype(BF16).astype(F32)
        ext[m, :HALO, :] = nn(tail, weights).astype(BF16).astype(F32)
    rows = lax.broadcasted_iota(jnp.int32, (count, count), 0)
    cols = lax.broadcasted_iota(jnp.int32, (count, count), 1)
    eye = (rows == cols).astype(F32)
    inclusive = (rows >= cols).astype(F32)
    strict = (rows > cols).astype(F32)
    log_gate = jnp.log(1.0 - 0.001 * gate_ref[...].astype(F32) / 1023.0)
    beta_rows = beta_ref[...].astype(F32) / 1023.0
    sums_row = nt(log_gate, inclusive, True)
    sums_col = nt(inclusive, log_gate, True)
    beta_cols = nt(eye, beta_rows, True)
    act = []
    for m in range(3):
        conv = cw_ref[m, 0:1, :] * ext[m, HALO - 3 : HALO - 3 + count, :]
        for j in range(1, KW):
            conv = conv + cw_ref[m, j : j + 1, :] * ext[m, HALO - 3 + j : HALO - 3 + j + count, :]
        sig = jax.nn.sigmoid(conv)
        act.append((conv * sig, sig * (1.0 + conv * (1.0 - sig))))
    out = []
    for h in range(heads):
        lanes = slice(h * DK, (h + 1) * DK)
        q_act, k_act, v = (act[m][0][:, lanes] for m in range(3))
        q_scale = lax.rsqrt(jnp.sum(q_act * q_act, -1, keepdims=True) + 1e-6)
        k_scale = lax.rsqrt(jnp.sum(k_act * k_act, -1, keepdims=True) + 1e-6)
        qn = q_act * q_scale
        s_col = sums_col[:, h : h + 1]
        beta = beta_cols[:, h : h + 1]
        total = s_col[count - 1 : count, :]
        d = dict(
            q=qn * DK**-0.5,
            k=k_act * k_scale,
            v=v,
            q_scale=q_scale * DK**-0.5,
            k_scale=k_scale,
            qn=qn,
            beta=beta,
            now=jnp.exp(s_col),
            rest=jnp.exp(total - s_col),
            whole=jnp.exp(total),
            g=g_ref[:, lanes].astype(F32),
            between=jnp.exp(s_col - sums_row[h : h + 1, :]),
        )
        d["low_scale"] = d["between"] * strict * beta
        d["between"] = d["between"] * inclusive
        out.append(d)
    for d in out:
        d["low"] = nt(d["k"], d["k"], True) * d["low_scale"]
    inverses = unit_inverses([d["low"] for d in out], eye, rows ^ cols)
    for d, inv in zip(out, inverses):
        d["inv"] = inv
        d["scores"] = nt(d["q"], d["k"]) * d["between"]
        d["k_rest"] = d["rest"] * d["k"]
        d["k_now"] = (d["beta"] * d["now"]) * d["k"]
        solved = nn(inv, jnp.concatenate([d["beta"] * d["v"], d["k_now"]], 1), True)
        d["u0"] = solved[:, :DK]
        d["kt"] = solved[:, DK:]
        both = tn(solved, d["k_rest"], True)
        d["B"] = both[:DK]
        d["A"] = d["whole"] * eye[:DK, :DK] - both[DK:]
        d["wg"] = tn(d["scores"], d["g"])
        d["C"] = tn(d["g"], d["now"] * d["q"]) - tn(d["wg"], d["kt"])
    return act, out


def carried_part(act, per_head, cw_ref, ext, grads, states):
    count = grads.shape[1] - 8
    parts = [[], [], []]
    for d, (start, arriving) in zip(per_head, states):
        u = d["u0"] - nt(d["kt"], start)
        du = d["wg"] + nt(d["k_rest"], arriving)
        y = tn(d["inv"], du)
        yg = jnp.concatenate([y, d["g"]], 0)
        outer = nt(yg, u)
        through = nn(yg, start)
        lows = jnp.concatenate(
            [-d["low_scale"] * outer[:count], d["between"] * outer[count:]], 0
        )
        by_rows = nn(lows, d["k"])
        by_cols = tn(lows, jnp.concatenate([d["k"], d["q"]], 0))
        dq = d["now"] * through[count:] + by_rows[count:]
        dk = (
            by_rows[:count]
            + by_cols
            - (d["beta"] * d["now"]) * through[:count]
            + d["rest"] * nn(u, arriving)
        )
        dq = d["q_scale"] * (dq - d["qn"] * jnp.sum(d["qn"] * dq, -1, keepdims=True))
        dk = d["k_scale"] * (dk - d["k"] * jnp.sum(d["k"] * dk, -1, keepdims=True))
        for m, part in enumerate((dq, dk, d["beta"] * y)):
            parts[m].append(part)
    tap_rows = []
    for m in range(3):
        dconv = jnp.concatenate(parts[m], 1) * act[m][1]
        grads[m, :count, :] = dconv
        for j in range(KW):
            tap_rows.append(
                jnp.sum(
                    dconv * ext[m, HALO - 3 + j : HALO - 3 + j + count, :], 0, keepdims=True
                )
            )
    return tap_rows


def raw_part(cw_ref, grads, m, count):
    raw = cw_ref[m, KW - 1 : KW, :] * grads[m, 0:count, :]
    for j in range(KW - 1):
        raw = raw + cw_ref[m, j : j + 1, :] * grads[m, KW - 1 - j : KW - 1 - j + count, :]
    return raw.astype(BF16)


def scan_states(get, me, ctx, heads):
    zero = jnp.zeros((DK, DK), F32)

    def step(i, carry):
        new = []
        back = ctx - 1 - i
        for h in range(heads):
            start, arriving = carry[h]
            keep_start = jnp.where(i < me, 1.0, 0.0)
            keep_back = jnp.where(back > me, 1.0, 0.0)
            start_next = nn(start, get(i, h, 0), True) + get(i, h, 1)
            back_next = nt(arriving, get(back, h, 0), True) + get(back, h, 2)
            new.append(
                (
                    keep_start * start_next + (1.0 - keep_start) * start,
                    keep_back * back_next + (1.0 - keep_back) * arriving,
                )
            )
        return tuple(new)

    return lax.fori_loop(0, ctx - 1, step, tuple((zero, zero) for _ in range(heads)))


def first_kernel(heads, tail, x, w, cw, gate, beta, g, mats, ext):
    _, out = local_part(tail[...], x, w, cw, gate, beta, g, ext, heads)
    for h, d in enumerate(out):
        for i, name in enumerate("ABC"):
            mats[h, i] = d[name]


def second_kernel(heads, ctx, tail, x, w, cw, gate, beta, g, mats, dconv, taps, ext, grads):
    me = lax.axis_index("ctx")
    act, out = local_part(tail[...], x, w, cw, gate, beta, g, ext, heads)
    states = scan_states(lambda i, h, n: mats[i, h, n], me, ctx, heads)
    tap_rows = carried_part(act, out, cw, ext, grads, states)
    for n, row in enumerate(tap_rows):
        taps[n : n + 1, :] = row
    dconv[...] = grads[:, : x.shape[0], :]


def third_kernel(w, cw, dconv, spill, out, grads):
    count = dconv.shape[1]
    grads[:, :count, :] = dconv[...]
    grads[:, count:, :] = spill[...]
    total = nt(raw_part(cw, grads, 0, count), w[0])
    for m in (1, 2):
        total = total + nt(raw_part(cw, grads, m, count), w[m])
    out[...] = total


def from_behind(block, axis, distance):
    devices = range(lax.axis_size(axis))
    route = [(i - distance, i) for i in devices if i - distance in devices]
    return lax.ppermute(block, axis, route)


def on_device(inputs, projection, conv_weight, gate_code, beta_code, grad_out):
    count = inputs.shape[0]
    heads = gate_code.shape[0]
    width = heads * DK
    ctx = lax.axis_size("ctx")
    params = pltpu.CompilerParams(vmem_limit_bytes=56 * 1024 * 1024)
    tail = from_behind(inputs[count - HALO :], "ctx", 1)
    ext = pltpu.VMEM((3, count + HALO, width), F32)
    grads = pltpu.VMEM((3, count + 8, width), F32)
    mats = pl.pallas_call(
        functools.partial(first_kernel, heads),
        out_shape=jax.ShapeDtypeStruct((heads, 3, DK, DK), F32),
        in_specs=[VMEM] * 7,
        out_specs=VMEM,
        scratch_shapes=[ext],
        compiler_params=params,
    )(tail, inputs, projection, conv_weight, gate_code, beta_code, grad_out)
    gathered = lax.all_gather(mats, "ctx")
    dconv, taps = pl.pallas_call(
        functools.partial(second_kernel, heads, ctx),
        out_shape=(
            jax.ShapeDtypeStruct((3, count, width), F32),
            jax.ShapeDtypeStruct((3 * KW, width), F32),
        ),
        in_specs=[VMEM] * 8,
        out_specs=(VMEM, VMEM),
        scratch_shapes=[ext, grads],
        compiler_params=params,
    )(tail, inputs, projection, conv_weight, gate_code, beta_code, grad_out, gathered)
    spill = from_behind(dconv[:, :8, :], "ctx", -1)
    partial = pl.pallas_call(
        third_kernel,
        out_shape=jax.ShapeDtypeStruct(inputs.shape, F32),
        in_specs=[VMEM] * 4,
        out_specs=VMEM,
        scratch_shapes=[grads],
        compiler_params=params,
    )(projection, conv_weight, dconv, spill)
    input_grad = lax.psum_scatter(partial, "head", scatter_dimension=0, tiled=True)
    kernel_grad = lax.psum(taps.reshape(3, KW, width), "ctx")
    return (input_grad.astype(BF16), kernel_grad)


def solution(mesh):
    return jax.shard_map(
        on_device,
        mesh=mesh,
        in_specs=(
            P("ctx", None),
            P(None, None, "head"),
            P(None, None, "head"),
            P("head", "ctx"),
            P("head", "ctx"),
            P("ctx", "head"),
        ),
        out_specs=(P(("ctx", "head"), None), P(None, None, "head")),
        check_vma=False,
    )
```

time: 484 us -> 156 us (0.32)
  other arithmetic: 167 us -> 1.69 us
  matrix products: 85.7 us -> 0 us
  waiting for transfers between devices: 140 us -> 68.8 us
  local copies, waits for them, and re-layouts: 33.2 us -> 2.84 us
  Pallas kernels: 0 us -> 27.6 us
    another operation x62 -> x0, other arithmetic: 152 us -> none  [the longest x45 151 us: block_step(): jax.scipy.linalg.solve_triangular(lower_part, target, lower=True, unit_di...]
    dot_general x110 -> x0, matrix products: 72.4 us -> none  [the longest x12 12.7 us: block_step(): jnp.einsum('hts,hsv->htv', scores, pseudo, precision=HIGHEST_PRECISION)]
    all_gather x4 -> x1, waiting for transfers between devices: 134 us -> 62.5 us  [on_device(): gathered = lax.all_gather(mats, 'ctx')]
    pallas_call x0 -> x3, Pallas kernels: none -> 27.6 us  [the longest x1 14.3 us: on_device(): pl.pallas_call(functools.partial(second_kernel, heads, ctx), out_shape=(j...]
    another operation x18 -> x0, matrix products: 13.3 us -> none  [block_step(): jax.scipy.linalg.solve_triangular(lower_part, target, lower=True, unit_di...]
    dynamic_slice x23 -> x0, local copies, waits for them, and re-layouts: 11.3 us -> none  [the longest x14 7.09 us: one(): lax.dynamic_index_in_dim(a, source, 0, False)]
  transfers between devices with their start and end apart: 7 -> 4, of which waited for: 5 -> 3; matrix products, arithmetic and copies ran while one was open for 24% -> 0% of each run, Pallas kernels for 0% -> 0%
where the time goes in v1:
time: 156 us
  waiting for transfers between devices  68.8 us (44%)
  blocking collectives  34.3 us (22%)
  Pallas kernels  27.6 us (18%)
  between operations  14.1 us (9%)
  starting transfers between devices  6.5 us (4%)
  local copies, waits for them, and re-layouts  2.84 us (2%)
  other arithmetic  1.69 us (1%)
    all_gather x1, waiting for transfers between devices, on_device(): gathered = lax.all_gather(mats, 'ctx')  62.5 us
    psum x1, blocking collectives, on_device(): kernel_grad = lax.psum(taps.reshape(3, KW, width), 'ctx')  34.3 us
    pallas_call x1, Pallas kernels, on_device(): pl.pallas_call(functools.partial(second_kernel, heads, ctx), out_shape=(j...  14.3 us
    pallas_call x1, Pallas kernels, on_device(): pl.pallas_call(functools.partial(first_kernel, heads), out_shape=jax.Shap...  8.86 us
    ppermute x2, waiting for transfers between devices, from_behind(): return lax.ppermute(block, axis, route)  6.31 us
    ppermute x2, starting transfers between devices, from_behind(): return lax.ppermute(block, axis, route)  6.25 us
    pallas_call x1, Pallas kernels, on_device(): pl.pallas_call(third_kernel, out_shape=jax.ShapeDtypeStruct(inputs.shape,...  4.37 us
  transfers between devices with their start and end apart: 4, of which 3 were waited for; matrix products, arithmetic and copies ran while one was open for 0% of the time, Pallas kernels for 0%

profile of v1, /device:TPU:0, one launch (start us, length us, event | category | flops | bytes accessed | tf_op | source)
XLA Modules:
  0.0 155.8 jit_solution(3573395484837450258)
XLA Ops:
  7.2 0.0 all-gather.3.cloned.1.call-start
  7.2 0.8 slice.6
  8.1 4.8 %collective-permute-start = (bf16[16,2048]{1,0:T(8,128)(2,1)S(1)}, bf16[16,2048]{1,0:T(8,128)(2,1)S(1)}, u32[]{:S(2)}, u32[]{:S(2)}) collective-permute-start(bf16[16,2048]{1,0:T(8,128)(2,1)S(1)} %slice.6), channel_id=1, source_target_pairs={{0,4},{4,8},{8,12},{12,16},{16,20},{20,24},{24,28},{1,5},{5,9},{9,... | collective-permute-start | bytes 196616 | tf_op jit(solution)/shard_map/ppermute | solution.py:221
  12.9 1.9 %collective-permute-done.tail = bf16[16,2048]{1,0:T(8,128)(2,1)S(1)} collective-permute-done((bf16[16,2048]{1,0:T(8,128)(2,1)S(1)}, bf16[16,2048]{1,0:T(8,128)(2,1)S(1)}, u32[]{:S(2)}, u32[]{:S(2)}) %collective-permute-start) | collective-permute-done | bytes 65568 | tf_op jit(solution)/shard_map/ppermute | solution.py:221
  14.8 0.0 copy-start
  14.8 0.6 copy-done
  15.4 8.9 %shard_map.77 = f32[2,3,128,128]{3,2,1,0:T(8,128)} custom-call(bf16[16,2048]{1,0:T(8,128)(2,1)} %copy-done, bf16[192,2048]{1,0:T(8,128)(2,1)} %x.3, bf16[3,2048,256]{2,1,0:T(8,128)(2,1)} %w.5, f32[3,4,256]{2,1,0:T(4,128)} %cw.5, s32[2,192]{1,0:T(2,128)} %gate.3, s32[2,192]{1,0:T(2,128)} %beta.3, bf16[192,256]{1,0:T(8,128)(2,1)} %g.3), custom_call_target="tpu_custom_call" | custom-call | tf_op jit(solution)/shard_map/pallas_call | solution.py:233
  24.3 0.0 all-gather.3.cloned.1.call-update
  24.3 0.2 reduce-scatter.2.cloned.1.call-start
  24.5 62.5 %all-gather.3.cloned.1.call-done = f32[16,3,128,128]{3,2,1,0:T(8,128)} async-done(((f32[2,3,128,128]{3,2,1,0:T(8,128)}), f32[16,3,128,128]{3,2,1,0:T(8,128)}) %all-gather.3.cloned.1.call-update) | async-done | bytes 3145744 | tf_op jit(solution)/shard_map/all_gather | solution.py:241
  87.0 14.3 %shard_map.78 = (f32[3,192,256]{2,1,0:T(8,128)}, f32[12,256]{1,0:T(8,128)}) custom-call(bf16[16,2048]{1,0:T(8,128)(2,1)} %copy-done, bf16[192,2048]{1,0:T(8,128)(2,1)} %x.3, bf16[3,2048,256]{2,1,0:T(8,128)(2,1)} %w.5, f32[3,4,256]{2,1,0:T(4,128)} %cw.5, s32[2,192]{1,0:T(2,128)} %gate.3, s32[2,192]{1,0:T(2,128)} %beta.3, bf16[192,256]{1,0:T(8,128)(2,1)} %g.3, ...), custom_call_target="tpu_custom_call" | custom-call | tf_op jit(solution)/shard_map/pallas_call | solution.py:242
  101.3 0.7 slice.7
  102.1 0.0 copy-start.2
  102.1 1.4 collective-permute-start.1
  103.5 4.4 %collective-permute-done.1.spill = f32[3,8,256]{2,1,0:T(8,128)S(1)} collective-permute-done((f32[3,8,256]{2,1,0:T(8,128)S(1)}, f32[3,8,256]{2,1,0:T(8,128)S(1)}, u32[]{:S(2)}, u32[]{:S(2)}) %collective-permute-start.1) | collective-permute-done | bytes 24608 | tf_op jit(solution)/shard_map/ppermute | solution.py:221
  107.9 0.0 copy-start.1
  107.9 0.6 copy-done.1
  108.5 4.4 %shard_map.79 = f32[192,2048]{1,0:T(8,128)} custom-call(bf16[3,2048,256]{2,1,0:T(8,128)(2,1)} %w.5, f32[3,4,256]{2,1,0:T(4,128)} %cw.5, f32[3,192,256]{2,1,0:T(8,128)} %get-tuple-element.4.dconv, f32[3,8,256]{2,1,0:T(8,128)} %copy-done.1), custom_call_target="tpu_custom_call" | custom-call | tf_op jit(solution)/shard_map/pallas_call | solution.py:254
  112.9 0.0 reduce-scatter.2.cloned.1.call-update
  112.9 0.0 copy-done.2
  113.0 34.3 %psum.7 = f32[3,4,256]{2,1,0:T(4,128)} all-reduce(f32[3,4,256]{2,1,0:T(4,128)S(1)} %reshape.7), channel_id=1, replica_groups=mesh['ctx'=8,'head'=4] {'ctx'}, use_global_device_ids=true, to_apply=%region_1.0 | all-reduce | flops 3072 | bytes 24576 | tf_op jit(solution)/shard_map/psum | solution.py:263
  147.3 0.0 reduce-scatter.2.cloned.1.call-done
  147.3 1.7 %convert_element_type.3 = bf16[48,2048]{1,0:T(8,128)(2,1)} convert(f32[48,2048]{1,0:T(8,128)} %reduce-scatter.2.cloned.1.call-done) | non-fusion elementwise | flops 98304 | bytes 589824 | tf_op jit(solution)/shard_map/convert_element_type | solution.py:264
  (1 shorter events, 0.0 us)
Async XLA Ops:
  7.2 79.9 %all-gather.3.cloned.1.call-start = ((), (), s32[]{:S(2)}) async-start(), calls=%async_computation.2 | async-start | bytes 3538944 | tf_op jit(solution)/shard_map/all_gather | solution.py:241
  8.1 6.7 %collective-permute-start = (bf16[16,2048]{1,0:T(8,128)(2,1)S(1)}, bf16[16,2048]{1,0:T(8,128)(2,1)S(1)}, u32[]{:S(2)}, u32[]{:S(2)}) collective-permute-start(bf16[16,2048]{1,0:T(8,128)(2,1)S(1)} %slice.6), channel_id=1, source_target_pairs={{0,4},{4,8},{8,12},{12,16},{16,20},{20,24},{24,28},{1,5},{5,9},{9,... | collective-permute-start | bytes 196616 | tf_op jit(solution)/shard_map/ppermute | solution.py:221
  14.8 0.6 copy-start
  24.3 123.0 %reduce-scatter.2.cloned.1.call-start = ((), (), s32[]{:S(2)}) async-start(), calls=%async_computation.1 | async-start | bytes 1966080 | tf_op jit(solution)/shard_map/reduce_scatter | solution.py:262
  102.1 10.8 %copy-start.2 = (f32[12,256]{1,0:T(8,128)S(1)}, f32[12,256]{1,0:T(8,128)}, u32[]{:S(2)}) copy-start(f32[12,256]{1,0:T(8,128)} %get-tuple-element.5) | copy-start | bytes 36868
  102.1 5.8 %collective-permute-start.1 = (f32[3,8,256]{2,1,0:T(8,128)S(1)}, f32[3,8,256]{2,1,0:T(8,128)S(1)}, u32[]{:S(2)}, u32[]{:S(2)}) collective-permute-start(f32[3,8,256]{2,1,0:T(8,128)S(1)} %slice.7), channel_id=1, source_target_pairs={{4,0},{8,4},{12,8},{16,12},{20,16},{24,20},{28,24},{5,1},{9,5},{13... | collective-permute-start | bytes 73736 | tf_op jit(solution)/shard_map/ppermute | solution.py:221
  107.9 0.6 copy-start.1
Sparse Core Ops, SparseCore 0:
  24.4 62.5 all-gather.2
  113.0 27.6 reduce-scatter.1

commit v2 on v1

v2 whole, which is shorter than its diff:
```python
import functools

import jax
import jax.numpy as jnp
from jax import lax
from jax.experimental import pallas as pl
from jax.experimental.pallas import tpu as pltpu
from jax.sharding import PartitionSpec as P

DK = 128
KW = 4
HALO = 16
F32 = jnp.float32
BF16 = jnp.bfloat16
VMEM = pl.BlockSpec(memory_space=pltpu.VMEM)


def contract(a, b, dims, precise):
    def one(left, right):
        return lax.dot_general(left, right, (dims, ((), ())), preferred_element_type=F32)

    if not precise:
        return one(a.astype(BF16), b.astype(BF16))
    a_high, b_high = a.astype(BF16), b.astype(BF16)
    total = one(a_high, b_high)
    if b.dtype == F32:
        total = total + one(a_high, (b - b_high.astype(F32)).astype(BF16))
    if a.dtype == F32:
        total = total + one((a - a_high.astype(F32)).astype(BF16), b_high)
    return total


def exact_nt(a, b):
    return lax.dot_general(
        a, b, (((1,), (1,)), ((), ())), precision=lax.Precision.HIGHEST, preferred_element_type=F32
    )


def nn(a, b, precise=False):
    return contract(a, b, ((1,), (0,)), precise)


def nt(a, b, precise=False):
    return contract(a, b, ((1,), (1,)), precise)


def tn(a, b, precise=False):
    return contract(a, b, ((0,), (0,)), precise)


def unit_inverses(lowers, eye, distance):
    count = eye.shape[0]
    inverses = [eye - jnp.where(distance == 1, low, 0.0) for low in lowers]
    size = 2
    while size < count:
        mask = (distance >= size) & (distance < 2 * size)
        inner = [nn(inv, jnp.where(mask, low, 0.0)) for inv, low in zip(inverses, lowers)]
        inverses = [inv - nn(mid, inv) for inv, mid in zip(inverses, inner)]
        size *= 2
    left = [eye - inv - nn(low, inv, True) for inv, low in zip(inverses, lowers)]
    return [inv + nn(inv, rest) for inv, rest in zip(inverses, left)]


def local_part(get_tail, x_ref, w_ref, cw_ref, gate_ref, beta_ref, g_ref, ext, heads):
    count = x_ref.shape[0]
    for m in range(3):
        ext[m, HALO:, :] = nn(x_ref[...], w_ref[m]).astype(BF16).astype(F32)
    tail = get_tail()
    for m in range(3):
        ext[m, :HALO, :] = nn(tail, w_ref[m]).astype(BF16).astype(F32)
    rows = lax.broadcasted_iota(jnp.int32, (count, count), 0)
    cols = lax.broadcasted_iota(jnp.int32, (count, count), 1)
    eye = (rows == cols).astype(F32)
    inclusive = (rows >= cols).astype(F32)
    strict = (rows > cols).astype(F32)
    log_gate = jnp.log(1.0 - 0.001 * gate_ref[...].astype(F32) / 1023.0)
    beta_rows = beta_ref[...].astype(F32) / 1023.0
    sums_row = exact_nt(log_gate, inclusive)
    sums_col = exact_nt(inclusive, log_gate)
    beta_cols = exact_nt(eye, beta_rows)
    act = []
    for m in range(3):
        conv = cw_ref[m, 0:1, :] * ext[m, HALO - 3 : HALO - 3 + count, :]
        for j in range(1, KW):
            conv = conv + cw_ref[m, j : j + 1, :] * ext[m, HALO - 3 + j : HALO - 3 + j + count, :]
        sig = jax.nn.sigmoid(conv)
        act.append((conv * sig, sig * (1.0 + conv * (1.0 - sig))))
    out = []
    for h in range(heads):
        lanes = slice(h * DK, (h + 1) * DK)
        q_act, k_act, v = (act[m][0][:, lanes] for m in range(3))
        q_scale = lax.rsqrt(jnp.sum(q_act * q_act, -1, keepdims=True) + 1e-6)
        k_scale = lax.rsqrt(jnp.sum(k_act * k_act, -1, keepdims=True) + 1e-6)
        qn = q_act * q_scale
        s_col = sums_col[:, h : h + 1]
        beta = beta_cols[:, h : h + 1]
        total = s_col[count - 1 : count, :]
        d = dict(
            q=qn * DK**-0.5,
            k=k_act * k_scale,
            v=v,
            q_scale=q_scale * DK**-0.5,
            k_scale=k_scale,
            qn=qn,
            beta=beta,
            now=jnp.exp(s_col),
            rest=jnp.exp(total - s_col),
            whole=jnp.exp(total),
            g=g_ref[:, lanes],
            between=jnp.exp(s_col - sums_row[h : h + 1, :]),
        )
        d["low_scale"] = d["between"] * strict * beta
        d["between"] = d["between"] * inclusive
        out.append(d)
    for d in out:
        d["low"] = nt(d["k"], d["k"], True) * d["low_scale"]
    inverses = unit_inverses([d["low"] for d in out], eye, rows ^ cols)
    for d, inv in zip(out, inverses):
        d["inv"] = inv
        d["scores"] = nt(d["q"], d["k"], True) * d["between"]
        d["k_rest"] = d["rest"] * d["k"]
        d["k_now"] = (d["beta"] * d["now"]) * d["k"]
        solved = nn(inv, jnp.concatenate([d["beta"] * d["v"], d["k_now"]], 1), True)
        d["u0"] = solved[:, :DK]
        d["kt"] = solved[:, DK:]
        both = tn(solved, d["k_rest"], True)
        d["B"] = both[:DK]
        d["A"] = d["whole"] * eye[:DK, :DK] - both[DK:]
        d["wg"] = tn(d["scores"], d["g"], True)
        d["C"] = tn(d["g"], d["now"] * d["q"], True) - tn(d["wg"], d["kt"], True)
    return act, out


def carried_part(act, per_head, cw_ref, ext, grads, states):
    count = grads.shape[1] - 8
    parts = [[], [], []]
    for d, (start, arriving) in zip(per_head, states):
        u = d["u0"] - nt(d["kt"], start, True)
        du = d["wg"] + nt(d["k_rest"], arriving, True)
        y = tn(d["inv"], du, True)
        yg = jnp.concatenate([y.astype(BF16), d["g"]], 0)
        outer = nt(yg, u)
        through = nn(yg, start)
        lows = jnp.concatenate(
            [-d["low_scale"] * outer[:count], d["between"] * outer[count:]], 0
        )
        by_rows = nn(lows, d["k"])
        by_cols = tn(lows, jnp.concatenate([d["k"], d["q"]], 0))
        dq = d["now"] * through[count:] + by_rows[count:]
        dk = (
            by_rows[:count]
            + by_cols
            - (d["beta"] * d["now"]) * through[:count]
            + d["rest"] * nn(u, arriving)
        )
        dq = d["q_scale"] * (dq - d["qn"] * jnp.sum(d["qn"] * dq, -1, keepdims=True))
        dk = d["k_scale"] * (dk - d["k"] * jnp.sum(d["k"] * dk, -1, keepdims=True))
        for m, part in enumerate((dq, dk, d["beta"] * y)):
            parts[m].append(part)
    for m in range(3):
        grads[m, :count, :] = jnp.concatenate(parts[m], 1) * act[m][1]


def tap_sums(ext, grads, taps):
    count = grads.shape[1] - 8
    for m in range(3):
        dconv = grads[m, :count, :]
        for j in range(KW):
            row = m * KW + j
            taps[row : row + 1, :] = jnp.sum(
                dconv * ext[m, HALO - 3 + j : HALO - 3 + j + count, :], 0, keepdims=True
            )
    taps[3 * KW :, :] = jnp.zeros((16 - 3 * KW, taps.shape[1]), F32)


def raw_part(cw_ref, grads, m, count):
    raw = cw_ref[m, KW - 1 : KW, :] * grads[m, 0:count, :]
    for j in range(KW - 1):
        raw = raw + cw_ref[m, j : j + 1, :] * grads[m, KW - 1 - j : KW - 1 - j + count, :]
    return raw.astype(BF16)


def whole_kernel(
    heads,
    x,
    w,
    cw,
    gate,
    beta,
    g,
    out,
    taps_out,
    ext,
    grads,
    tail,
    spill,
    pair_out,
    pair_in,
    chain_out,
    chain_in,
    taps,
    rounded,
    partial_out,
    partial_in,
    tail_sems,
    spill_sems,
    pair_sems,
    chain_send,
    chain_recv,
    taps_send,
    taps_recv,
    partial_send,
    partial_recv,
):
    count, depth = x.shape
    ctx, head_axis = lax.axis_size("ctx"), lax.axis_size("head")
    me, head_me = lax.axis_index("ctx"), lax.axis_index("head")
    pairs = ctx // 2
    place, odd = me // 2, me % 2

    def send(src, dst, send_sem, recv_sem, axis, target):
        return pltpu.make_async_remote_copy(
            src_ref=src,
            dst_ref=dst,
            send_sem=send_sem,
            recv_sem=recv_sem,
            device_id={axis: target},
            device_id_type=pl.DeviceIdType.MESH,
        )

    barrier = pltpu.get_barrier_semaphore()
    for axis, at, size in (("ctx", me, ctx), ("head", head_me, head_axis)):
        for d in range(1, size):
            pl.semaphore_signal(
                barrier,
                inc=1,
                device_id={axis: (at + d) % size},
                device_id_type=pl.DeviceIdType.MESH,
            )
    pl.semaphore_wait(barrier, ctx + head_axis - 2)

    tail_copy = send(
        x.at[count - HALO :], tail, tail_sems.at[0], tail_sems.at[1], "ctx", (me + 1) % ctx
    )
    tail_copy.start()

    def get_tail():
        tail_copy.wait()
        return jnp.where(me == 0, jnp.zeros_like(tail), tail[...])

    act, per_head = local_part(get_tail, x, w, cw, gate, beta, g, ext, heads)
    for h, d in enumerate(per_head):
        for i, name in enumerate("ABC"):
            pair_out[h, i] = d[name].astype(BF16)
    pair_copy = send(
        pair_out, pair_in, pair_sems.at[0], pair_sems.at[1], "ctx", me + 1 - 2 * odd
    )
    pair_copy.start()
    pair_copy.wait()
    is_odd = odd == 1
    early, late, merged = [], [], []
    for h, d in enumerate(per_head):
        own = [d[name] for name in "ABC"]
        other = [pair_in[h, i].astype(F32) for i in range(3)]
        first = [jnp.where(is_odd, o, m) for m, o in zip(own, other)]
        second = [jnp.where(is_odd, m, o) for m, o in zip(own, other)]
        early.append(first)
        late.append(second)
        merged.append(
            (
                nn(first[0], second[0], True),
                nn(first[1], second[0], True) + second[1],
                nt(second[2], first[0], True) + first[2],
            )
        )

    forward_copy = send(
        chain_out.at[0], chain_in.at[0], chain_send.at[0], chain_recv.at[0], "ctx", (me + 2) % ctx
    )
    backward_copy = send(
        chain_out.at[1],
        chain_in.at[1],
        chain_send.at[1],
        chain_recv.at[1],
        "ctx",
        (me + ctx - 2) % ctx,
    )

    def forward():
        @pl.when(place == 0)
        def _():
            chain_in[0] = jnp.zeros_like(chain_in[0])

        @pl.when(place > 0)
        def _():
            forward_copy.wait_recv()

        @pl.when(place < pairs - 1)
        def _():
            for h in range(heads):
                chain_out[0, h] = (
                    nn(chain_in[0, h], merged[h][0], True) + merged[h][1]
                ).astype(BF16)
            forward_copy.start()

    def backward():
        @pl.when(place == pairs - 1)
        def _():
            chain_in[1] = jnp.zeros_like(chain_in[1])

        @pl.when(place < pairs - 1)
        def _():
            backward_copy.wait_recv()

        @pl.when(place > 0)
        def _():
            for h in range(heads):
                chain_out[1, h] = (
                    nt(chain_in[1, h], merged[h][0], True) + merged[h][2]
                ).astype(BF16)
            backward_copy.start()

    @pl.when(place < pairs // 2)
    def _():
        forward()
        backward()

    @pl.when(place >= pairs // 2)
    def _():
        backward()
        forward()

    states = []
    for h in range(heads):
        start, arriving = chain_in[0, h], chain_in[1, h]
        start_odd = nn(start, early[h][0], True) + early[h][1]
        arriving_even = nt(arriving, late[h][0], True) + late[h][2]
        states.append(
            (
                jnp.where(is_odd, start_odd, start.astype(F32)),
                jnp.where(is_odd, arriving.astype(F32), arriving_even),
            )
        )
    carried_part(act, per_head, cw, ext, grads, states)
    spill_copy = send(
        grads.at[:, 0:8, :], spill, spill_sems.at[0], spill_sems.at[1], "ctx", (me + ctx - 1) % ctx
    )
    spill_copy.start()
    tap_sums(ext, grads, taps.at[me])
    taps_copies = [
        send(
            taps.at[me],
            taps.at[me],
            taps_send.at[d - 1],
            taps_recv.at[d - 1],
            "ctx",
            (me + d) % ctx,
        )
        for d in range(1, ctx)
    ]
    for copy in taps_copies:
        copy.start()
    spill_copy.wait()
    grads[:, count:, :] = jnp.where(me == ctx - 1, jnp.zeros_like(spill), spill[...])
    width = w.shape[2]
    for m in range(3):
        rounded[:, m * width : (m + 1) * width] = raw_part(cw, grads, m, count)
    block = count // head_axis
    chunks, _, span = partial_out.shape
    own = []
    copies = []
    for c in range(chunks):
        total = None
        for m in range(3):
            term = nt(
                rounded[:, m * width : (m + 1) * width], w[m, c * span : (c + 1) * span, :]
            )
            total = term if total is None else total + term
        partial_out[c] = total.astype(BF16)
        for d in (2, 1, 3) if head_axis == 4 else range(1, head_axis):
            target = (head_me + d) % head_axis
            copy = send(
                partial_out.at[c, pl.ds(pl.multiple_of(target * block, 16), block)],
                partial_in.at[d - 1, c],
                partial_send.at[d - 1, c],
                partial_recv.at[d - 1, c],
                "head",
                target,
            )
            copy.start()
            copies.append(copy)
    for copy in taps_copies:
        copy.wait()
    summed = taps[0]
    for i in range(1, ctx):
        summed = summed + taps[i]
    taps_out[...] = summed[: 3 * KW]
    for copy in copies:
        copy.wait()
    for c in range(chunks):
        total = partial_out[c, pl.ds(pl.multiple_of(head_me * block, 16), block), :].astype(F32)
        for d in range(1, head_axis):
            total = total + partial_in[d - 1, c].astype(F32)
        out[:, c * span : (c + 1) * span] = total.astype(BF16)

    @pl.when(place < pairs - 1)
    def _():
        forward_copy.wait_send()

    @pl.when(place > 0)
    def _():
        backward_copy.wait_send()


def on_device(inputs, projection, conv_weight, gate_code, beta_code, grad_out):
    count, depth = inputs.shape
    heads = gate_code.shape[0]
    width = heads * DK
    ctx, head_axis = lax.axis_size("ctx"), lax.axis_size("head")
    chunks = 4
    span = depth // chunks
    block = count // head_axis
    dma = pltpu.SemaphoreType.DMA
    input_grad, taps = pl.pallas_call(
        functools.partial(whole_kernel, heads),
        out_shape=(
            jax.ShapeDtypeStruct((block, depth), BF16),
            jax.ShapeDtypeStruct((3 * KW, width), F32),
        ),
        in_specs=[VMEM] * 6,
        out_specs=(VMEM, VMEM),
        scratch_shapes=[
            pltpu.VMEM((3, count + HALO, width), F32),
            pltpu.VMEM((3, count + 8, width), F32),
            pltpu.VMEM((HALO, depth), BF16),
            pltpu.VMEM((3, 8, width), F32),
            pltpu.VMEM((heads, 3, DK, DK), BF16),
            pltpu.VMEM((heads, 3, DK, DK), BF16),
            pltpu.VMEM((2, heads, DK, DK), BF16),
            pltpu.VMEM((2, heads, DK, DK), BF16),
            pltpu.VMEM((ctx, 16, width), F32),
            pltpu.VMEM((count, 3 * width), BF16),
            pltpu.VMEM((chunks, count, span), BF16),
            pltpu.VMEM((head_axis - 1, chunks, block, span), BF16),
            dma((2,)),
            dma((2,)),
            dma((2,)),
            dma((2,)),
            dma((2,)),
            dma((ctx - 1,)),
            dma((ctx - 1,)),
            dma((head_axis - 1, chunks)),
            dma((head_axis - 1, chunks)),
        ],
        compiler_params=pltpu.CompilerParams(
            collective_id=0, has_side_effects=True, vmem_limit_bytes=56 * 1024 * 1024
        ),
    )(inputs, projection, conv_weight, gate_code, beta_code, grad_out)
    return (input_grad, taps.reshape(3, KW, width))


def solution(mesh):
    return jax.shard_map(
        on_device,
        mesh=mesh,
        in_specs=(
            P("ctx", None),
            P(None, None, "head"),
            P(None, None, "head"),
            P("head", "ctx"),
            P("head", "ctx"),
            P("ctx", "head"),
        ),
        out_specs=(P(("ctx", "head"), None), P(None, None, "head")),
        check_vma=False,
    )
```

time: 156 us -> 48.5 us (0.31)
  waiting for transfers between devices: 68.8 us -> 0 us
  blocking collectives: 34.3 us -> 0 us
  Pallas kernels: 27.6 us -> 44.6 us
  between operations: 14.1 us -> 0.64 us
  starting transfers between devices: 6.5 us -> 0 us
  other arithmetic: 1.69 us -> 0 us
    all_gather x1 -> x0, waiting for transfers between devices: 62.5 us -> none  [on_device(): gathered = lax.all_gather(mats, 'ctx')]
    psum x1 -> x0, blocking collectives: 34.3 us -> none  [on_device(): kernel_grad = lax.psum(taps.reshape(3, KW, width), 'ctx')]
    pallas_call x3 -> x1, Pallas kernels: 27.6 us -> 44.6 us  [on_device(): pl.pallas_call(functools.partial(whole_kernel, heads), out_shape=(jax.Sha...]
    ppermute x2 -> x0, waiting for transfers between devices: 6.31 us -> none  [from_behind(): return lax.ppermute(block, axis, route)]
    ppermute x2 -> x0, starting transfers between devices: 6.25 us -> none  [from_behind(): return lax.ppermute(block, axis, route)]
    convert_element_type x1 -> x0, other arithmetic: 1.69 us -> none  [on_device(): return (input_grad.astype(BF16), kernel_grad)]
    slice x2 -> x0, local copies, waits for them, and re-layouts: 1.59 us -> none  [the longest x1 0.85 us: on_device(): tail = from_behind(inputs[count - HALO:], 'ctx', 1)]
  transfers between devices with their start and end apart: 4 -> 0, of which waited for: 3 -> 0; matrix products, arithmetic and copies ran while one was open for 0% -> 0% of each run, Pallas kernels for 0% -> 0%
where the time goes in v2:
time: 48.5 us; the launch traced here: 48.2 us
  Pallas kernels  44.6 us (92%)
  local copies, waits for them, and re-layouts  2.94 us (6%)
  between operations  0.64 us (1%)
    pallas_call x1, Pallas kernels, on_device(): pl.pallas_call(functools.partial(whole_kernel, heads), out_shape=(jax.Sha...  44.6 us
    unnamed x1, local copies, waits for them, and re-layouts  1.62 us
    reshape x1, local copies, waits for them, and re-layouts, on_device(): return (input_grad, taps.reshape(3, KW, width))  1.33 us

profile of v2, /device:TPU:0, one launch (start us, length us, event | category | flops | bytes accessed | tf_op | source)
XLA Modules:
  0.0 48.2 jit_solution(18392140247937131373)
XLA Ops:
  0.6 44.6 %shard_map.77 = (bf16[48,2048]{1,0:T(8,128)(2,1)}, f32[12,256]{1,0:T(8,128)}) custom-call(bf16[192,2048]{1,0:T(8,128)(2,1)} %x.1, bf16[3,2048,256]{2,1,0:T(8,128)(2,1)} %w.1, f32[3,4,256]{2,1,0:T(4,128)} %cw.1, s32[2,192]{1,0:T(2,128)} %gate.1, s32[2,192]{1,0:T(2,128)} %beta.1, bf16[192,256]{1,0:T(8,128)(2,1)} %g.1), custom_call_target="tpu_custom_call" | custom-call | tf_op jit(solution)/shard_map/pallas_call | solution.py:424
  45.3 1.3 %reshape.7 = f32[3,4,256]{2,1,0:T(4,128)} reshape(f32[12,256]{1,0:T(8,128)} %get-tuple-element.5) | data formatting | bytes 24576 | tf_op jit(solution)/shard_map/reshape | solution.py:459
  46.6 1.6 %copy.9 = bf16[48,2048]{1,0:T(8,128)(2,1)} copy(bf16[48,2048]{1,0:T(8,128)(2,1)} %get-tuple-element.8) | data formatting | bytes 393216

commit v3 on v2

--- a/solution.py
+++ b/solution.py
@@ -13,6 +13,7 @@
 F32 = jnp.float32
 BF16 = jnp.bfloat16
 VMEM = pl.BlockSpec(memory_space=pltpu.VMEM)
+ANY = pl.BlockSpec(memory_space=pl.ANY)
 
 
 def contract(a, b, dims, precise):
@@ -61,9 +62,10 @@
     return [inv + nn(inv, rest) for inv, rest in zip(inverses, left)]
 
 
-def local_part(get_tail, x_ref, w_ref, cw_ref, gate_ref, beta_ref, g_ref, ext, heads):
+def local_part(get_weights, get_tail, x_ref, w_ref, cw_ref, gate_ref, beta_ref, g_ref, ext, heads):
     count = x_ref.shape[0]
-    for m in range(3):
+    for m in (1, 0, 2):
+        get_weights(m)
         ext[m, HALO:, :] = nn(x_ref[...], w_ref[m]).astype(BF16).astype(F32)
     tail = get_tail()
     for m in range(3):
@@ -136,8 +138,7 @@
     parts = [[], [], []]
     for d, (start, arriving) in zip(per_head, states):
         u = d["u0"] - nt(d["kt"], start, True)
-        du = d["wg"] + nt(d["k_rest"], arriving, True)
-        y = tn(d["inv"], du, True)
+        y = d["y0"] + nt(d["kt_rest"], arriving, True)
         yg = jnp.concatenate([y.astype(BF16), d["g"]], 0)
         outer = nt(yg, u)
         through = nn(yg, start)
@@ -182,14 +183,16 @@
 
 def whole_kernel(
     heads,
-    x,
-    w,
+    x_hbm,
+    w_hbm,
     cw,
     gate,
     beta,
     g,
     out,
     taps_out,
+    x,
+    w,
     ext,
     grads,
     tail,
@@ -200,17 +203,24 @@
     chain_in,
     taps,
     rounded,
-    partial_out,
-    partial_in,
+    total,
+    near_out,
+    near_in,
+    far_out,
+    far_in,
+    load_sems,
     tail_sems,
     spill_sems,
-    pair_sems,
+    pair_send,
+    pair_recv,
     chain_send,
     chain_recv,
     taps_send,
     taps_recv,
-    partial_send,
-    partial_recv,
+    near_send,
+    near_recv,
+    far_send,
+    far_recv,
 ):
     count, depth = x.shape
     ctx, head_axis = lax.axis_size("ctx"), lax.axis_size("head")
@@ -228,6 +238,10 @@
             device_id_type=pl.DeviceIdType.MESH,
         )
 
+    loads = [pltpu.make_async_copy(w_hbm.at[m], w.at[m], load_sems.at[m]) for m in range(3)]
+    loads.append(pltpu.make_async_copy(x_hbm, x, load_sems.at[3]))
+    for m in (3, 1, 0, 2):
+        loads[m].start()
     barrier = pltpu.get_barrier_semaphore()
     for axis, at, size in (("ctx", me, ctx), ("head", head_me, head_axis)):
         for d in range(1, size):
@@ -240,7 +254,7 @@
     pl.semaphore_wait(barrier, ctx + head_axis - 2)
 
     tail_copy = send(
-        x.at[count - HALO :], tail, tail_sems.at[0], tail_sems.at[1], "ctx", (me + 1) % ctx
+        x_hbm.at[count - HALO :], tail, tail_sems.at[0], tail_sems.at[1], "ctx", (me + 1) % ctx
     )
     tail_copy.start()
 
@@ -248,18 +262,33 @@
         tail_copy.wait()
         return jnp.where(me == 0, jnp.zeros_like(tail), tail[...])
 
-    act, per_head = local_part(get_tail, x, w, cw, gate, beta, g, ext, heads)
+    def get_weights(m):
+        loads[m].wait()
+
+    loads[3].wait()
+    act, per_head = local_part(get_weights, get_tail, x, w, cw, gate, beta, g, ext, heads)
+    pair_copies = []
     for h, d in enumerate(per_head):
         for i, name in enumerate("ABC"):
             pair_out[h, i] = d[name].astype(BF16)
-    pair_copy = send(
-        pair_out, pair_in, pair_sems.at[0], pair_sems.at[1], "ctx", me + 1 - 2 * odd
-    )
-    pair_copy.start()
-    pair_copy.wait()
+        pair_copies.append(
+            send(
+                pair_out.at[h],
+                pair_in.at[h],
+                pair_send.at[h],
+                pair_recv.at[h],
+                "ctx",
+                me + 1 - 2 * odd,
+            )
+        )
+        pair_copies[h].start()
+    for d in per_head:
+        back = tn(d["inv"], jnp.concatenate([d["wg"], d["k_rest"]], 1), True)
+        d["y0"], d["kt_rest"] = back[:, :DK], back[:, DK:]
     is_odd = odd == 1
     early, late, merged = [], [], []
     for h, d in enumerate(per_head):
+        pair_copies[h].wait()
         own = [d[name] for name in "ABC"]
         other = [pair_in[h, i].astype(F32) for i in range(3)]
         first = [jnp.where(is_odd, o, m) for m, o in zip(own, other)]
@@ -274,51 +303,64 @@
             )
         )
 
-    forward_copy = send(
-        chain_out.at[0], chain_in.at[0], chain_send.at[0], chain_recv.at[0], "ctx", (me + 2) % ctx
-    )
-    backward_copy = send(
-        chain_out.at[1],
-        chain_in.at[1],
-        chain_send.at[1],
-        chain_recv.at[1],
-        "ctx",
-        (me + ctx - 2) % ctx,
-    )
+    forward_copies, backward_copies = [], []
+    for h in range(heads):
+        forward_copies.append(
+            send(
+                chain_out.at[0, h],
+                chain_in.at[0, h],
+                chain_send.at[0, h],
+                chain_recv.at[0, h],
+                "ctx",
+                (me + 2) % ctx,
+            )
+        )
+        backward_copies.append(
+            send(
+                chain_out.at[1, h],
+                chain_in.at[1, h],
+                chain_send.at[1, h],
+                chain_recv.at[1, h],
+                "ctx",
+                (me + ctx - 2) % ctx,
+            )
+        )
 
     def forward():
         @pl.when(place == 0)
         def _():
             chain_in[0] = jnp.zeros_like(chain_in[0])
 
-        @pl.when(place > 0)
-        def _():
-            forward_copy.wait_recv()
-
-        @pl.when(place < pairs - 1)
-        def _():
-            for h in range(heads):
+        for h in range(heads):
+
+            @pl.when(place > 0)
+            def _():
+                forward_copies[h].wait_recv()
+
+            @pl.when(place < pairs - 1)
+            def _():
                 chain_out[0, h] = (
                     nn(chain_in[0, h], merged[h][0], True) + merged[h][1]
                 ).astype(BF16)
-            forward_copy.start()
+                forward_copies[h].start()
 
     def backward():
         @pl.when(place == pairs - 1)
         def _():
             chain_in[1] = jnp.zeros_like(chain_in[1])
 
-        @pl.when(place < pairs - 1)
-        def _():
-            backward_copy.wait_recv()
-
-        @pl.when(place > 0)
-        def _():
-            for h in range(heads):
+        for h in range(heads):
+
+            @pl.when(place < pairs - 1)
+            def _():
+                backward_copies[h].wait_recv()
+
+            @pl.when(place > 0)
+            def _():
                 chain_out[1, h] = (
                     nt(chain_in[1, h], merged[h][0], True) + merged[h][2]
                 ).astype(BF16)
-            backward_copy.start()
+                backward_copies[h].start()
 
     @pl.when(place < pairs // 2)
     def _():
@@ -366,50 +408,76 @@
     for m in range(3):
         rounded[:, m * width : (m + 1) * width] = raw_part(cw, grads, m, count)
     block = count // head_axis
-    chunks, _, span = partial_out.shape
-    own = []
-    copies = []
+    chunks, _, span = total.shape
+    sibling = head_me + 1 - 2 * (head_me % 2)
+    far = (head_me + 2) % 4
+
+    def rows_of(c, owner):
+        return total[c, pl.ds(pl.multiple_of(owner * block, 16), block), :]
+
+    near_copies, far_copies = [], []
+
+    def pass_on(c):
+        near_copies[c].wait_recv()
+        far_out[c] = (rows_of(c, far) + near_in[c, block:].astype(F32)).astype(BF16)
+        copy = send(
+            far_out.at[c], far_in.at[c], far_send.at[c], far_recv.at[c], "head", far
+        )
+        copy.start()
+        far_copies.append(copy)
+
     for c in range(chunks):
-        total = None
+        part = None
         for m in range(3):
             term = nt(
                 rounded[:, m * width : (m + 1) * width], w[m, c * span : (c + 1) * span, :]
             )
-            total = term if total is None else total + term
-        partial_out[c] = total.astype(BF16)
-        for d in (2, 1, 3) if head_axis == 4 else range(1, head_axis):
-            target = (head_me + d) % head_axis
-            copy = send(
-                partial_out.at[c, pl.ds(pl.multiple_of(target * block, 16), block)],
-                partial_in.at[d - 1, c],
-                partial_send.at[d - 1, c],
-                partial_recv.at[d - 1, c],
-                "head",
-                target,
-            )
-            copy.start()
-            copies.append(copy)
+            part = term if part is None else part + term
+        total[c] = part
+        near_out[c, :block] = rows_of(c, sibling).astype(BF16)
+        near_out[c, block:] = rows_of(c, (sibling + 2) % 4).astype(BF16)
+        copy = send(
+            near_out.at[c], near_in.at[c], near_send.at[c], near_recv.at[c], "head", sibling
+        )
+        copy.start()
+        near_copies.append(copy)
+        if c > 0:
+            pass_on(c - 1)
+    pass_on(chunks - 1)
     for copy in taps_copies:
         copy.wait()
     summed = taps[0]
     for i in range(1, ctx):
         summed = summed + taps[i]
-    taps_out[...] = summed[: 3 * KW]
+    for m in range(3):
+        taps_out[m] = summed[m * KW : (m + 1) * KW]
+    for c in range(chunks):
+        far_copies[c].wait_recv()
+        result = rows_of(c, head_me) + near_in[c, :block].astype(F32) + far_in[c].astype(F32)
+        out[:, c * span : (c + 1) * span] = result.astype(BF16)
+    for copy in near_copies + far_copies:
+        copy.wait_send()
+
+    @pl.when(place < pairs - 1)
+    def _():
+        for copy in forward_copies:
+            copy.wait_send()
+
+    @pl.when(place > 0)
+    def _():
+        for copy in backward_copies:
+            copy.wait_send()
+
+
+def store_kernel(grad, taps, grad_out, taps_out, sems):
+    copies = [
+        pltpu.make_async_copy(grad, grad_out, sems.at[0]),
+        pltpu.make_async_copy(taps, taps_out, sems.at[1]),
+    ]
+    for copy in copies:
+        copy.start()
     for copy in copies:
         copy.wait()
-    for c in range(chunks):
-        total = partial_out[c, pl.ds(pl.multiple_of(head_me * block, 16), block), :].astype(F32)
-        for d in range(1, head_axis):
-            total = total + partial_in[d - 1, c].astype(F32)
-        out[:, c * span : (c + 1) * span] = total.astype(BF16)
-
-    @pl.when(place < pairs - 1)
-    def _():
-        forward_copy.wait_send()
-
-    @pl.when(place > 0)
-    def _():
-        backward_copy.wait_send()
 
 
 def on_device(inputs, projection, conv_weight, gate_code, beta_code, grad_out):
@@ -425,11 +493,13 @@
         functools.partial(whole_kernel, heads),
         out_shape=(
             jax.ShapeDtypeStruct((block, depth), BF16),
-            jax.ShapeDtypeStruct((3 * KW, width), F32),
+            jax.ShapeDtypeStruct((3, KW, width), F32),
         ),
-        in_specs=[VMEM] * 6,
+        in_specs=[ANY, ANY] + [VMEM] * 4,
         out_specs=(VMEM, VMEM),
         scratch_shapes=[
+            pltpu.VMEM(inputs.shape, BF16),
+            pltpu.VMEM(projection.shape, BF16),
             pltpu.VMEM((3, count + HALO, width), F32),
             pltpu.VMEM((3, count + 8, width), F32),
             pltpu.VMEM((HALO, depth), BF16),
@@ -440,23 +510,39 @@
             pltpu.VMEM((2, heads, DK, DK), BF16),
             pltpu.VMEM((ctx, 16, width), F32),
             pltpu.VMEM((count, 3 * width), BF16),
-            pltpu.VMEM((chunks, count, span), BF16),
-            pltpu.VMEM((head_axis - 1, chunks, block, span), BF16),
+            pltpu.VMEM((chunks, count, span), F32),
+            pltpu.VMEM((chunks, 2 * block, span), BF16),
+            pltpu.VMEM((chunks, 2 * block, span), BF16),
+            pltpu.VMEM((chunks, block, span), BF16),
+            pltpu.VMEM((chunks, block, span), BF16),
+            dma((4,)),
             dma((2,)),
             dma((2,)),
-            dma((2,)),
-            dma((2,)),
-            dma((2,)),
+            dma((heads,)),
+            dma((heads,)),
+            dma((2, heads)),
+            dma((2, heads)),
             dma((ctx - 1,)),
             dma((ctx - 1,)),
-            dma((head_axis - 1, chunks)),
-            dma((head_axis - 1, chunks)),
+            dma((chunks,)),
+            dma((chunks,)),
+            dma((chunks,)),
+            dma((chunks,)),
         ],
         compiler_params=pltpu.CompilerParams(
             collective_id=0, has_side_effects=True, vmem_limit_bytes=56 * 1024 * 1024
         ),
     )(inputs, projection, conv_weight, gate_code, beta_code, grad_out)
-    return (input_grad, taps.reshape(3, KW, width))
+    return pl.pallas_call(
+        store_kernel,
+        out_shape=(
+            jax.ShapeDtypeStruct((block, depth), BF16),
+            jax.ShapeDtypeStruct((3, KW, width), F32),
+        ),
+        in_specs=[ANY, ANY],
+        out_specs=(ANY, ANY),
+        scratch_shapes=[dma((2,))],
+    )(input_grad, taps)
 
 
 def solution(mesh):

time: 48.5 us -> 51 us (1.052)
  Pallas kernels: 44.6 us -> 50.2 us
  local copies, waits for them, and re-layouts: 2.94 us -> 0 us
    pallas_call x0 -> x1, Pallas kernels: none -> 7.45 us  [on_device(): pl.pallas_call(store_kernel, out_shape=(jax.ShapeDtypeStruct((block, dept...]
    pallas_call x1, Pallas kernels: 44.6 us -> 42.7 us  [on_device(): pl.pallas_call(functools.partial(whole_kernel, heads), out_shape=(jax.Sha...]
    unnamed x1 -> x0, local copies, waits for them, and re-layouts: 1.62 us -> none
    reshape x1 -> x0, local copies, waits for them, and re-layouts: 1.33 us -> none  [on_device(): return (input_grad, taps.reshape(3, KW, width))]
where the time goes in v3:
time: 51 us; the launch traced here: 50.8 us
  Pallas kernels  50.2 us (98%)
  between operations  0.64 us (1%)
    pallas_call x1, Pallas kernels, on_device(): pl.pallas_call(functools.partial(whole_kernel, heads), out_shape=(jax.Sha...  42.7 us
    pallas_call x1, Pallas kernels, on_device(): pl.pallas_call(store_kernel, out_shape=(jax.ShapeDtypeStruct((block, dept...  7.45 us

profile of v3, /device:TPU:0, one launch (start us, length us, event | category | flops | bytes accessed | tf_op | source)
XLA Modules:
  0.0 50.8 jit_solution(2534195608879869828)
XLA Ops:
  0.6 42.7 %shard_map.77 = (bf16[48,2048]{1,0:T(8,128)(2,1)}, f32[3,4,256]{2,1,0:T(4,128)}) custom-call(bf16[192,2048]{1,0:T(8,128)(2,1)} %x_hbm.1, bf16[3,2048,256]{2,1,0:T(8,128)(2,1)} %w_hbm.1, f32[3,4,256]{2,1,0:T(4,128)} %cw.1, s32[2,192]{1,0:T(2,128)} %gate.1, s32[2,192]{1,0:T(2,128)} %beta.1, bf16[192,256]{1,0:T(8,128)(2,1)} %g.1), custom_call_target="tpu_custom_call" | custom-call | tf_op jit(solution)/shard_map/pallas_call | solution.py:492
  43.4 7.4 %shard_map.78 = (bf16[48,2048]{1,0:T(8,128)(2,1)}, f32[3,4,256]{2,1,0:T(4,128)}) custom-call(bf16[48,2048]{1,0:T(8,128)(2,1)} %get-tuple-element.4.grad, f32[3,4,256]{2,1,0:T(4,128)} %get-tuple-element.5.taps), custom_call_target="tpu_custom_call" | custom-call | tf_op jit(solution)/shard_map/pallas_call | solution.py:536

commit v4 on v3

--- a/solution.py
+++ b/solution.py
@@ -9,6 +9,7 @@
 
 DK = 128
 KW = 4
+GROUP = 64
 HALO = 16
 F32 = jnp.float32
 BF16 = jnp.bfloat16
@@ -62,7 +63,27 @@
     return [inv + nn(inv, rest) for inv, rest in zip(inverses, left)]
 
 
-def local_part(get_weights, get_tail, x_ref, w_ref, cw_ref, gate_ref, beta_ref, g_ref, ext, heads):
+def solve_down(d, rows):
+    done = []
+    for b, inv in enumerate(d["inv"]):
+        part = rows[b * GROUP : (b + 1) * GROUP]
+        if b > 0:
+            part = part - nn(d["off"][b], jnp.concatenate(done, 0), True)
+        done.append(nn(inv, part, True))
+    return jnp.concatenate(done, 0)
+
+
+def solve_up(d, rows):
+    done = []
+    for b in reversed(range(len(d["inv"]))):
+        part = tn(d["inv"][b], rows[b * GROUP : (b + 1) * GROUP], True)
+        done.insert(0, part)
+        if b > 0:
+            rows = rows[: b * GROUP] - tn(d["off"][b], part, True)
+    return jnp.concatenate(done, 0)
+
+
+def local_part(get_weights, get_tail, x_ref, w_ref, cw_ref, gate_ref, beta_ref, g_ref, ext, slope, heads):
     count = x_ref.shape[0]
     for m in (1, 0, 2):
         get_weights(m)
@@ -86,11 +107,12 @@
         for j in range(1, KW):
             conv = conv + cw_ref[m, j : j + 1, :] * ext[m, HALO - 3 + j : HALO - 3 + j + count, :]
         sig = jax.nn.sigmoid(conv)
-        act.append((conv * sig, sig * (1.0 + conv * (1.0 - sig))))
+        act.append(conv * sig)
+        slope[m] = conv
     out = []
     for h in range(heads):
         lanes = slice(h * DK, (h + 1) * DK)
-        q_act, k_act, v = (act[m][0][:, lanes] for m in range(3))
+        q_act, k_act, v = (act[m][:, lanes] for m in range(3))
         q_scale = lax.rsqrt(jnp.sum(q_act * q_act, -1, keepdims=True) + 1e-6)
         k_scale = lax.rsqrt(jnp.sum(k_act * k_act, -1, keepdims=True) + 1e-6)
         qn = q_act * q_scale
@@ -109,57 +131,95 @@
             rest=jnp.exp(total - s_col),
             whole=jnp.exp(total),
             g=g_ref[:, lanes],
-            between=jnp.exp(s_col - sums_row[h : h + 1, :]),
-        )
-        d["low_scale"] = d["between"] * strict * beta
-        d["between"] = d["between"] * inclusive
+        )
+        d["s_col"], d["s_row"] = s_col, sums_row[h : h + 1, :]
+        d["beta_row"] = beta_rows[h : h + 1, :]
+        d["low"], d["off"] = [], []
+        for b in range(count // GROUP):
+            here, before = slice(b * GROUP, (b + 1) * GROUP), slice(0, b * GROUP)
+            keys = d["k"][here]
+            scale = jnp.exp(s_col[here] - d["s_row"][:, here]) * strict[:GROUP, :GROUP]
+            d["low"].append(nt(keys, keys, True) * (scale * beta[here]))
+            if b > 0:
+                scale = jnp.exp(s_col[here] - d["s_row"][:, before]) * beta[here]
+                d["off"].append(nt(keys, d["k"][before], True) * scale)
+            else:
+                d["off"].append(None)
         out.append(d)
-    for d in out:
-        d["low"] = nt(d["k"], d["k"], True) * d["low_scale"]
-    inverses = unit_inverses([d["low"] for d in out], eye, rows ^ cols)
-    for d, inv in zip(out, inverses):
-        d["inv"] = inv
-        d["scores"] = nt(d["q"], d["k"], True) * d["between"]
+    blocks = count // GROUP
+    inverses = unit_inverses(
+        [low for d in out for low in d["low"]],
+        eye[:GROUP, :GROUP],
+        rows[:GROUP, :GROUP] ^ cols[:GROUP, :GROUP],
+    )
+    for h, d in enumerate(out):
+        d["inv"] = inverses[h * blocks : (h + 1) * blocks]
         d["k_rest"] = d["rest"] * d["k"]
         d["k_now"] = (d["beta"] * d["now"]) * d["k"]
-        solved = nn(inv, jnp.concatenate([d["beta"] * d["v"], d["k_now"]], 1), True)
+        solved = solve_down(d, jnp.concatenate([d["beta"] * d["v"], d["k_now"]], 1))
         d["u0"] = solved[:, :DK]
         d["kt"] = solved[:, DK:]
         both = tn(solved, d["k_rest"], True)
         d["B"] = both[:DK]
         d["A"] = d["whole"] * eye[:DK, :DK] - both[DK:]
+    return out
+
+
+def adjoint_part(per_head):
+    for d in per_head:
+        count = d["k"].shape[0]
+        rows = lax.broadcasted_iota(jnp.int32, (count, count), 0)
+        cols = lax.broadcasted_iota(jnp.int32, (count, count), 1)
+        decay = jnp.exp(d["s_col"] - d["s_row"])
+        d["between"] = jnp.where(rows >= cols, decay, 0.0)
+        d["scores"] = nt(d["q"], d["k"], True) * d["between"]
         d["wg"] = tn(d["scores"], d["g"], True)
         d["C"] = tn(d["g"], d["now"] * d["q"], True) - tn(d["wg"], d["kt"], True)
-    return act, out
-
-
-def carried_part(act, per_head, cw_ref, ext, grads, states):
+
+
+def prepared_part(per_head, slope):
+    for m in range(3):
+        sig = jax.nn.sigmoid(slope[m])
+        slope[m] = sig * (1.0 + slope[m] * (1.0 - sig))
+    for d in per_head:
+        count = d["k"].shape[0]
+        back = solve_up(d, jnp.concatenate([d["wg"], d["k_rest"]], 1))
+        d["y0"], d["kt_rest"] = back[:, :DK], back[:, DK:]
+        rows = lax.broadcasted_iota(jnp.int32, (count, count), 0)
+        cols = lax.broadcasted_iota(jnp.int32, (count, count), 1)
+        d["low_scale"] = jnp.where(rows > cols, -d["beta"] * d["between"], 0.0)
+        turned = jnp.exp(d["s_row"] - d["s_col"])
+        d["between_t"] = jnp.where(rows <= cols, turned, 0.0)
+        d["low_scale_t"] = jnp.where(rows < cols, -d["beta_row"] * turned, 0.0)
+
+
+def carried_part(per_head, slope, grads, states):
     count = grads.shape[1] - 8
     parts = [[], [], []]
     for d, (start, arriving) in zip(per_head, states):
         u = d["u0"] - nt(d["kt"], start, True)
         y = d["y0"] + nt(d["kt_rest"], arriving, True)
-        yg = jnp.concatenate([y.astype(BF16), d["g"]], 0)
-        outer = nt(yg, u)
-        through = nn(yg, start)
-        lows = jnp.concatenate(
-            [-d["low_scale"] * outer[:count], d["between"] * outer[count:]], 0
-        )
-        by_rows = nn(lows, d["k"])
-        by_cols = tn(lows, jnp.concatenate([d["k"], d["q"]], 0))
-        dq = d["now"] * through[count:] + by_rows[count:]
+        keys, asks = d["k"].astype(BF16), d["q"].astype(BF16)
+        u_low, y_low = u.astype(BF16), y.astype(BF16)
+        start_low, arriving_low = start.astype(BF16), arriving.astype(BF16)
+        low = d["low_scale"] * nt(y_low, u_low)
+        low_t = d["low_scale_t"] * nt(u_low, y_low)
+        seen = d["between"] * nt(d["g"], u_low)
+        seen_t = d["between_t"] * nt(u_low, d["g"])
+        dq = d["now"] * nn(d["g"], start_low) + nn(seen, keys)
         dk = (
-            by_rows[:count]
-            + by_cols
-            - (d["beta"] * d["now"]) * through[:count]
-            + d["rest"] * nn(u, arriving)
+            nn(low, keys)
+            + nn(low_t, keys)
+            + nn(seen_t, asks)
+            - (d["beta"] * d["now"]) * nn(y_low, start_low)
+            + d["rest"] * nn(u_low, arriving_low)
         )
         dq = d["q_scale"] * (dq - d["qn"] * jnp.sum(d["qn"] * dq, -1, keepdims=True))
         dk = d["k_scale"] * (dk - d["k"] * jnp.sum(d["k"] * dk, -1, keepdims=True))
         for m, part in enumerate((dq, dk, d["beta"] * y)):
             parts[m].append(part)
     for m in range(3):
-        grads[m, :count, :] = jnp.concatenate(parts[m], 1) * act[m][1]
+        grads[m, :count, :] = jnp.concatenate(parts[m], 1) * slope[m]
 
 
 def tap_sums(ext, grads, taps):
@@ -174,10 +234,11 @@
     taps[3 * KW :, :] = jnp.zeros((16 - 3 * KW, taps.shape[1]), F32)
 
 
-def raw_part(cw_ref, grads, m, count):
-    raw = cw_ref[m, KW - 1 : KW, :] * grads[m, 0:count, :]
+def raw_part(cw_ref, grads, m, at, count):
+    raw = cw_ref[m, KW - 1 : KW, :] * grads[m, at : at + count, :]
     for j in range(KW - 1):
-        raw = raw + cw_ref[m, j : j + 1, :] * grads[m, KW - 1 - j : KW - 1 - j + count, :]
+        first = at + KW - 1 - j
+        raw = raw + cw_ref[m, j : j + 1, :] * grads[m, first : first + count, :]
     return raw.astype(BF16)
 
 
@@ -194,6 +255,7 @@
     x,
     w,
     ext,
+    slope,
     grads,
     tail,
     spill,
@@ -266,29 +328,35 @@
         loads[m].wait()
 
     loads[3].wait()
-    act, per_head = local_part(get_weights, get_tail, x, w, cw, gate, beta, g, ext, heads)
+    per_head = local_part(get_weights, get_tail, x, w, cw, gate, beta, g, ext, slope, heads)
     pair_copies = []
-    for h, d in enumerate(per_head):
-        for i, name in enumerate("ABC"):
-            pair_out[h, i] = d[name].astype(BF16)
-        pair_copies.append(
-            send(
-                pair_out.at[h],
-                pair_in.at[h],
-                pair_send.at[h],
-                pair_recv.at[h],
-                "ctx",
-                me + 1 - 2 * odd,
-            )
-        )
-        pair_copies[h].start()
-    for d in per_head:
-        back = tn(d["inv"], jnp.concatenate([d["wg"], d["k_rest"]], 1), True)
-        d["y0"], d["kt_rest"] = back[:, :DK], back[:, DK:]
+
+    def send_pair(h, first, names):
+        for i, name in enumerate(names):
+            pair_out[h, first + i] = per_head[h][name].astype(BF16)
+        part = pl.ds(first, len(names))
+        copy = send(
+            pair_out.at[h, part],
+            pair_in.at[h, part],
+            pair_send.at[h, first // 2],
+            pair_recv.at[h, first // 2],
+            "ctx",
+            me + 1 - 2 * odd,
+        )
+        copy.start()
+        pair_copies.append(copy)
+
+    for h in range(heads):
+        send_pair(h, 0, "AB")
+    adjoint_part(per_head)
+    for h in range(heads):
+        send_pair(h, 2, "C")
+    prepared_part(per_head, slope)
     is_odd = odd == 1
     early, late, merged = [], [], []
     for h, d in enumerate(per_head):
         pair_copies[h].wait()
+        pair_copies[heads + h].wait()
         own = [d[name] for name in "ABC"]
         other = [pair_in[h, i].astype(F32) for i in range(3)]
         first = [jnp.where(is_odd, o, m) for m, o in zip(own, other)]
@@ -383,7 +451,7 @@
                 jnp.where(is_odd, arriving.astype(F32), arriving_even),
             )
         )
-    carried_part(act, per_head, cw, ext, grads, states)
+    carried_part(per_head, slope, grads, states)
     spill_copy = send(
         grads.at[:, 0:8, :], spill, spill_sems.at[0], spill_sems.at[1], "ctx", (me + ctx - 1) % ctx
     )
@@ -402,13 +470,28 @@
     ]
     for copy in taps_copies:
         copy.start()
+    width = w.shape[2]
+    edge = count - 16
+    chunks, _, span = total.shape
+
+    def product(c, rows):
+        part = None
+        for m in range(3):
+            term = nt(
+                rounded[rows, m * width : (m + 1) * width], w[m, c * span : (c + 1) * span, :]
+            )
+            part = term if part is None else part + term
+        total[c, rows] = part
+
+    for m in range(3):
+        rounded[:edge, m * width : (m + 1) * width] = raw_part(cw, grads, m, 0, edge)
+    product(0, slice(0, edge))
     spill_copy.wait()
     grads[:, count:, :] = jnp.where(me == ctx - 1, jnp.zeros_like(spill), spill[...])
-    width = w.shape[2]
-    for m in range(3):
-        rounded[:, m * width : (m + 1) * width] = raw_part(cw, grads, m, count)
+    for m in range(3):
+        rounded[edge:, m * width : (m + 1) * width] = raw_part(cw, grads, m, edge, 16)
+    product(0, slice(edge, count))
     block = count // head_axis
-    chunks, _, span = total.shape
     sibling = head_me + 1 - 2 * (head_me % 2)
     far = (head_me + 2) % 4
 
@@ -427,13 +510,8 @@
         far_copies.append(copy)
 
     for c in range(chunks):
-        part = None
-        for m in range(3):
-            term = nt(
-                rounded[:, m * width : (m + 1) * width], w[m, c * span : (c + 1) * span, :]
-            )
-            part = term if part is None else part + term
-        total[c] = part
+        if c > 0:
+            product(c, slice(0, count))
         near_out[c, :block] = rows_of(c, sibling).astype(BF16)
         near_out[c, block:] = rows_of(c, (sibling + 2) % 4).astype(BF16)
         copy = send(
@@ -469,15 +547,9 @@
             copy.wait_send()
 
 
-def store_kernel(grad, taps, grad_out, taps_out, sems):
-    copies = [
-        pltpu.make_async_copy(grad, grad_out, sems.at[0]),
-        pltpu.make_async_copy(taps, taps_out, sems.at[1]),
-    ]
-    for copy in copies:
-        copy.start()
-    for copy in copies:
-        copy.wait()
+def store_kernel(grad, taps, grad_out, taps_out):
+    grad_out[...] = grad[...]
+    taps_out[...] = taps[...]
 
 
 def on_device(inputs, projection, conv_weight, gate_code, beta_code, grad_out):
@@ -501,6 +573,7 @@
             pltpu.VMEM(inputs.shape, BF16),
             pltpu.VMEM(projection.shape, BF16),
             pltpu.VMEM((3, count + HALO, width), F32),
+            pltpu.VMEM((3, count, width), F32),
             pltpu.VMEM((3, count + 8, width), F32),
             pltpu.VMEM((HALO, depth), BF16),
             pltpu.VMEM((3, 8, width), F32),
@@ -518,8 +591,8 @@
             dma((4,)),
             dma((2,)),
             dma((2,)),
-            dma((heads,)),
-            dma((heads,)),
+            dma((heads, 2)),
+            dma((heads, 2)),
             dma((2, heads)),
             dma((2, heads)),
             dma((ctx - 1,)),
@@ -539,9 +612,8 @@
             jax.ShapeDtypeStruct((block, depth), BF16),
             jax.ShapeDtypeStruct((3, KW, width), F32),
         ),
-        in_specs=[ANY, ANY],
-        out_specs=(ANY, ANY),
-        scratch_shapes=[dma((2,))],
+        in_specs=[VMEM, VMEM],
+        out_specs=(VMEM, VMEM),
     )(input_grad, taps)
 
 

time: 51 us -> 45.4 us (0.89)
  Pallas kernels: 50.2 us -> 44.6 us
    pallas_call x1, Pallas kernels: 7.45 us -> 1.62 us  [on_device(): pl.pallas_call(store_kernel, out_shape=(jax.ShapeDtypeStruct((block, dept...]
where the time goes in v4:
time: 45.4 us; the launch traced here: 45.2 us
  Pallas kernels  44.6 us (98%)
  between operations  0.64 us (1%)
    pallas_call x1, Pallas kernels, on_device(): pl.pallas_call(functools.partial(whole_kernel, heads), out_shape=(jax.Sha...  42.9 us
    pallas_call x1, Pallas kernels, on_device(): pl.pallas_call(store_kernel, out_shape=(jax.ShapeDtypeStruct((block, dept...  1.62 us

profile of v4, /device:TPU:0, one launch (start us, length us, event | category | flops | bytes accessed | tf_op | source)
XLA Modules:
  0.0 45.2 jit_solution(14942321890091790885)
XLA Ops:
  0.6 42.9 %shard_map.77 = (bf16[48,2048]{1,0:T(8,128)(2,1)}, f32[3,4,256]{2,1,0:T(4,128)}) custom-call(bf16[192,2048]{1,0:T(8,128)(2,1)} %x_hbm.1, bf16[3,2048,256]{2,1,0:T(8,128)(2,1)} %w_hbm.1, f32[3,4,256]{2,1,0:T(4,128)} %cw.1, s32[2,192]{1,0:T(2,128)} %gate.1, s32[2,192]{1,0:T(2,128)} %beta.1, bf16[192,256]{1,0:T(8,128)(2,1)} %g.1), custom_call_target="tpu_custom_call" | custom-call | tf_op jit(solution)/shard_map/pallas_call | solution.py:564
  43.6 1.6 %shard_map.78 = (bf16[48,2048]{1,0:T(8,128)(2,1)}, f32[3,4,256]{2,1,0:T(4,128)}) custom-call(bf16[48,2048]{1,0:T(8,128)(2,1)} %get-tuple-element.4.grad, f32[3,4,256]{2,1,0:T(4,128)} %get-tuple-element.5.taps), custom_call_target="tpu_custom_call" | custom-call | tf_op jit(solution)/shard_map/pallas_call | solution.py:609

commit v5 on v4

--- a/solution.py
+++ b/solution.py
@@ -88,6 +88,8 @@
     for m in (1, 0, 2):
         get_weights(m)
         ext[m, HALO:, :] = nn(x_ref[...], w_ref[m]).astype(BF16).astype(F32)
+    for n in range(4, 8):
+        get_weights(n)
     tail = get_tail()
     for m in range(3):
         ext[m, :HALO, :] = nn(tail, w_ref[m]).astype(BF16).astype(F32)
@@ -146,6 +148,10 @@
             else:
                 d["off"].append(None)
         out.append(d)
+    for d in out:
+        d["between"] = jnp.exp(d["s_col"] - d["s_row"]) * inclusive
+        d["scores"] = nt(d["q"], d["k"], True) * d["between"]
+        d["wg"] = tn(d["scores"], d["g"], True)
     blocks = count // GROUP
     inverses = unit_inverses(
         [low for d in out for low in d["low"]],
@@ -162,19 +168,8 @@
         both = tn(solved, d["k_rest"], True)
         d["B"] = both[:DK]
         d["A"] = d["whole"] * eye[:DK, :DK] - both[DK:]
+        d["C"] = tn(d["g"], d["now"] * d["q"], True) - tn(d["wg"], d["kt"], True)
     return out
-
-
-def adjoint_part(per_head):
-    for d in per_head:
-        count = d["k"].shape[0]
-        rows = lax.broadcasted_iota(jnp.int32, (count, count), 0)
-        cols = lax.broadcasted_iota(jnp.int32, (count, count), 1)
-        decay = jnp.exp(d["s_col"] - d["s_row"])
-        d["between"] = jnp.where(rows >= cols, decay, 0.0)
-        d["scores"] = nt(d["q"], d["k"], True) * d["between"]
-        d["wg"] = tn(d["scores"], d["g"], True)
-        d["C"] = tn(d["g"], d["now"] * d["q"], True) - tn(d["wg"], d["kt"], True)
 
 
 def prepared_part(per_head, slope):
@@ -246,14 +241,19 @@
     heads,
     x_hbm,
     w_hbm,
+    cw_hbm,
+    gate_hbm,
+    beta_hbm,
+    g_hbm,
+    out,
+    taps_out,
+    x,
+    w,
     cw,
     gate,
     beta,
     g,
-    out,
-    taps_out,
-    x,
-    w,
+    merged,
     ext,
     slope,
     grads,
@@ -301,9 +301,9 @@
         )
 
     loads = [pltpu.make_async_copy(w_hbm.at[m], w.at[m], load_sems.at[m]) for m in range(3)]
-    loads.append(pltpu.make_async_copy(x_hbm, x, load_sems.at[3]))
-    for m in (3, 1, 0, 2):
-        loads[m].start()
+    others = ((x_hbm, x), (cw_hbm, cw), (gate_hbm, gate), (beta_hbm, beta), (g_hbm, g))
+    for n, (src, dst) in enumerate(others):
+        loads.append(pltpu.make_async_copy(src, dst, load_sems.at[3 + n]))
     barrier = pltpu.get_barrier_semaphore()
     for axis, at, size in (("ctx", me, ctx), ("head", head_me, head_axis)):
         for d in range(1, size):
@@ -313,6 +313,8 @@
                 device_id={axis: (at + d) % size},
                 device_id_type=pl.DeviceIdType.MESH,
             )
+    for m in (3, 1, 0, 2, 4, 5, 6, 7):
+        loads[m].start()
     pl.semaphore_wait(barrier, ctx + head_axis - 2)
 
     tail_copy = send(
@@ -331,45 +333,48 @@
     per_head = local_part(get_weights, get_tail, x, w, cw, gate, beta, g, ext, slope, heads)
     pair_copies = []
 
-    def send_pair(h, first, names):
-        for i, name in enumerate(names):
-            pair_out[h, first + i] = per_head[h][name].astype(BF16)
-        part = pl.ds(first, len(names))
-        copy = send(
-            pair_out.at[h, part],
-            pair_in.at[h, part],
-            pair_send.at[h, first // 2],
-            pair_recv.at[h, first // 2],
-            "ctx",
-            me + 1 - 2 * odd,
-        )
-        copy.start()
-        pair_copies.append(copy)
-
-    for h in range(heads):
-        send_pair(h, 0, "AB")
-    adjoint_part(per_head)
-    for h in range(heads):
-        send_pair(h, 2, "C")
+    half = place < pairs // 2
+    for h, d in enumerate(per_head):
+        pair_out[h, 0] = d["A"].astype(BF16)
+        pair_out[h, 1] = jnp.where(half, d["B"], d["C"]).astype(BF16)
+        pair_out[h, 2] = jnp.where(half, d["C"], d["B"]).astype(BF16)
+    for n, part in enumerate((pl.ds(0, 2), pl.ds(2, 1))):
+        for h in range(heads):
+            copy = send(
+                pair_out.at[h, part],
+                pair_in.at[h, part],
+                pair_send.at[h, n],
+                pair_recv.at[h, n],
+                "ctx",
+                me + 1 - 2 * odd,
+            )
+            copy.start()
+            pair_copies.append(copy)
     prepared_part(per_head, slope)
     is_odd = odd == 1
-    early, late, merged = [], [], []
-    for h, d in enumerate(per_head):
-        pair_copies[h].wait()
-        pair_copies[heads + h].wait()
-        own = [d[name] for name in "ABC"]
-        other = [pair_in[h, i].astype(F32) for i in range(3)]
-        first = [jnp.where(is_odd, o, m) for m, o in zip(own, other)]
-        second = [jnp.where(is_odd, m, o) for m, o in zip(own, other)]
-        early.append(first)
-        late.append(second)
-        merged.append(
-            (
-                nn(first[0], second[0], True),
-                nn(first[1], second[0], True) + second[1],
-                nt(second[2], first[0], True) + first[2],
-            )
-        )
+
+    def ordered(h, name, slot):
+        own, other = per_head[h][name], pair_in[h, slot].astype(F32)
+        return jnp.where(is_odd, other, own), jnp.where(is_odd, own, other)
+
+    def merge_forward(slot):
+        for h in range(heads):
+            (_, a_late), (b_early, b_late) = ordered(h, "A", 0), ordered(h, "B", slot)
+            merged[h, 1] = nn(b_early, a_late, True) + b_late
+
+    def merge_backward(slot):
+        for h in range(heads):
+            (a_early, _), (c_early, c_late) = ordered(h, "A", 0), ordered(h, "C", slot)
+            merged[h, 2] = nt(c_late, a_early, True) + c_early
+
+    def wait_rest():
+        for copy in pair_copies[heads:]:
+            copy.wait_recv()
+
+    for h in range(heads):
+        pair_copies[h].wait_recv()
+        a_early, a_late = ordered(h, "A", 0)
+        merged[h, 0] = nn(a_early, a_late, True)
 
     forward_copies, backward_copies = [], []
     for h in range(heads):
@@ -408,7 +413,7 @@
             @pl.when(place < pairs - 1)
             def _():
                 chain_out[0, h] = (
-                    nn(chain_in[0, h], merged[h][0], True) + merged[h][1]
+                    nn(chain_in[0, h], merged[h, 0], True) + merged[h, 1]
                 ).astype(BF16)
                 forward_copies[h].start()
 
@@ -426,25 +431,36 @@
             @pl.when(place > 0)
             def _():
                 chain_out[1, h] = (
-                    nt(chain_in[1, h], merged[h][0], True) + merged[h][2]
+                    nt(chain_in[1, h], merged[h, 0], True) + merged[h, 2]
                 ).astype(BF16)
                 backward_copies[h].start()
 
-    @pl.when(place < pairs // 2)
+    @pl.when(half)
     def _():
+        merge_forward(1)
         forward()
+        wait_rest()
+        merge_backward(2)
         backward()
 
     @pl.when(place >= pairs // 2)
     def _():
+        merge_backward(1)
         backward()
+        wait_rest()
+        merge_forward(2)
         forward()
 
     states = []
     for h in range(heads):
         start, arriving = chain_in[0, h], chain_in[1, h]
-        start_odd = nn(start, early[h][0], True) + early[h][1]
-        arriving_even = nt(arriving, late[h][0], True) + late[h][2]
+        a_early, a_late = ordered(h, "A", 0)
+        other_b = jnp.where(half, pair_in[h, 1], pair_in[h, 2]).astype(F32)
+        other_c = jnp.where(half, pair_in[h, 2], pair_in[h, 1]).astype(F32)
+        b_early = jnp.where(is_odd, other_b, per_head[h]["B"])
+        c_late = jnp.where(is_odd, per_head[h]["C"], other_c)
+        start_odd = nn(start, a_early, True) + b_early
+        arriving_even = nt(arriving, a_late, True) + c_late
         states.append(
             (
                 jnp.where(is_odd, start_odd, start.astype(F32)),
@@ -533,7 +549,7 @@
         far_copies[c].wait_recv()
         result = rows_of(c, head_me) + near_in[c, :block].astype(F32) + far_in[c].astype(F32)
         out[:, c * span : (c + 1) * span] = result.astype(BF16)
-    for copy in near_copies + far_copies:
+    for copy in near_copies + far_copies + pair_copies:
         copy.wait_send()
 
     @pl.when(place < pairs - 1)
@@ -567,11 +583,16 @@
             jax.ShapeDtypeStruct((block, depth), BF16),
             jax.ShapeDtypeStruct((3, KW, width), F32),
         ),
-        in_specs=[ANY, ANY] + [VMEM] * 4,
+        in_specs=[ANY] * 6,
         out_specs=(VMEM, VMEM),
         scratch_shapes=[
             pltpu.VMEM(inputs.shape, BF16),
             pltpu.VMEM(projection.shape, BF16),
+            pltpu.VMEM(conv_weight.shape, F32),
+            pltpu.VMEM(gate_code.shape, jnp.int32),
+            pltpu.VMEM(beta_code.shape, jnp.int32),
+            pltpu.VMEM(grad_out.shape, BF16),
+            pltpu.VMEM((heads, 3, DK, DK), F32),
             pltpu.VMEM((3, count + HALO, width), F32),
             pltpu.VMEM((3, count, width), F32),
             pltpu.VMEM((3, count + 8, width), F32),
@@ -588,7 +609,7 @@
             pltpu.VMEM((chunks, 2 * block, span), BF16),
             pltpu.VMEM((chunks, block, span), BF16),
             pltpu.VMEM((chunks, block, span), BF16),
-            dma((4,)),
+            dma((8,)),
             dma((2,)),
             dma((2,)),
             dma((heads, 2)),

time: 45.4 us -> 46.6 us (1.026)
  Pallas kernels: 44.6 us -> 45.8 us
    pallas_call x1, Pallas kernels: 42.9 us -> 44.1 us  [on_device(): pl.pallas_call(functools.partial(whole_kernel, heads), out_shape=(jax.Sha...]
where the time goes in v5:
time: 46.6 us; the launch traced here: 46.4 us
  Pallas kernels  45.8 us (98%)
  between operations  0.64 us (1%)
    pallas_call x1, Pallas kernels, on_device(): pl.pallas_call(functools.partial(whole_kernel, heads), out_shape=(jax.Sha...  44.1 us
    pallas_call x1, Pallas kernels, on_device(): pl.pallas_call(store_kernel, out_shape=(jax.ShapeDtypeStruct((block, dept...  1.62 us

profile of v5, /device:TPU:0, one launch (start us, length us, event | category | flops | bytes accessed | tf_op | source)
XLA Modules:
  0.0 46.4 jit_solution(3710860824660616344)
XLA Ops:
  0.6 44.1 %shard_map.77 = (bf16[48,2048]{1,0:T(8,128)(2,1)}, f32[3,4,256]{2,1,0:T(4,128)}) custom-call(bf16[192,2048]{1,0:T(8,128)(2,1)} %x_hbm.1, bf16[3,2048,256]{2,1,0:T(8,128)(2,1)} %w_hbm.1, f32[3,4,256]{2,1,0:T(4,128)} %cw_hbm.1, s32[2,192]{1,0:T(2,128)} %gate_hbm.1, s32[2,192]{1,0:T(2,128)} %beta_hbm.1, bf16[192,256]{1,0:T(8,128)(2,1)} %g_hbm.1), custom_call_target="tpu_custom_call" | custom-call | tf_op jit(solution)/shard_map/pallas_call | solution.py:580
  44.8 1.6 %shard_map.78 = (bf16[48,2048]{1,0:T(8,128)(2,1)}, f32[3,4,256]{2,1,0:T(4,128)}) custom-call(bf16[48,2048]{1,0:T(8,128)(2,1)} %get-tuple-element.4.grad, f32[3,4,256]{2,1,0:T(4,128)} %get-tuple-element.5.taps), custom_call_target="tpu_custom_call" | custom-call | tf_op jit(solution)/shard_map/pallas_call | solution.py:630

commit v6 on v5

--- a/solution.py
+++ b/solution.py
@@ -148,10 +148,6 @@
             else:
                 d["off"].append(None)
         out.append(d)
-    for d in out:
-        d["between"] = jnp.exp(d["s_col"] - d["s_row"]) * inclusive
-        d["scores"] = nt(d["q"], d["k"], True) * d["between"]
-        d["wg"] = tn(d["scores"], d["g"], True)
     blocks = count // GROUP
     inverses = unit_inverses(
         [low for d in out for low in d["low"]],
@@ -168,8 +164,17 @@
         both = tn(solved, d["k_rest"], True)
         d["B"] = both[:DK]
         d["A"] = d["whole"] * eye[:DK, :DK] - both[DK:]
+    return out
+
+
+def adjoint_part(per_head):
+    for d in per_head:
+        count = d["k"].shape[0]
+        rows = lax.broadcasted_iota(jnp.int32, (count, count), 0)
+        cols = lax.broadcasted_iota(jnp.int32, (count, count), 1)
+        d["between_t"] = jnp.where(rows <= cols, jnp.exp(d["s_row"] - d["s_col"]), 0.0)
+        d["wg"] = nn(nt(d["k"], d["q"], True) * d["between_t"], d["g"], True)
         d["C"] = tn(d["g"], d["now"] * d["q"], True) - tn(d["wg"], d["kt"], True)
-    return out
 
 
 def prepared_part(per_head, slope):
@@ -182,10 +187,10 @@
         d["y0"], d["kt_rest"] = back[:, :DK], back[:, DK:]
         rows = lax.broadcasted_iota(jnp.int32, (count, count), 0)
         cols = lax.broadcasted_iota(jnp.int32, (count, count), 1)
-        d["low_scale"] = jnp.where(rows > cols, -d["beta"] * d["between"], 0.0)
-        turned = jnp.exp(d["s_row"] - d["s_col"])
-        d["between_t"] = jnp.where(rows <= cols, turned, 0.0)
-        d["low_scale_t"] = jnp.where(rows < cols, -d["beta_row"] * turned, 0.0)
+        decay = jnp.exp(d["s_col"] - d["s_row"])
+        d["between"] = jnp.where(rows >= cols, decay, 0.0)
+        d["low_scale"] = jnp.where(rows > cols, -d["beta"] * decay, 0.0)
+        d["low_scale_t"] = jnp.where(rows < cols, -d["beta_row"] * d["between_t"], 0.0)
 
 
 def carried_part(per_head, slope, grads, states):
@@ -304,6 +309,8 @@
     others = ((x_hbm, x), (cw_hbm, cw), (gate_hbm, gate), (beta_hbm, beta), (g_hbm, g))
     for n, (src, dst) in enumerate(others):
         loads.append(pltpu.make_async_copy(src, dst, load_sems.at[3 + n]))
+    for m in (3, 1, 0, 2, 4, 5, 6, 7):
+        loads[m].start()
     barrier = pltpu.get_barrier_semaphore()
     for axis, at, size in (("ctx", me, ctx), ("head", head_me, head_axis)):
         for d in range(1, size):
@@ -313,8 +320,6 @@
                 device_id={axis: (at + d) % size},
                 device_id_type=pl.DeviceIdType.MESH,
             )
-    for m in (3, 1, 0, 2, 4, 5, 6, 7):
-        loads[m].start()
     pl.semaphore_wait(barrier, ctx + head_axis - 2)
 
     tail_copy = send(
@@ -331,25 +336,46 @@
 
     loads[3].wait()
     per_head = local_part(get_weights, get_tail, x, w, cw, gate, beta, g, ext, slope, heads)
-    pair_copies = []
-
     half = place < pairs // 2
+    pair_copies = {
+        (h, i): send(
+            pair_out.at[h, i],
+            pair_in.at[h, i],
+            pair_send.at[h, i],
+            pair_recv.at[h, i],
+            "ctx",
+            me + 1 - 2 * odd,
+        )
+        for h in range(heads)
+        for i in range(3)
+    }
+
+    def start_pair(i):
+        for h in range(heads):
+            pair_copies[h, i].start()
+
+    def wait_pair(i):
+        for h in range(heads):
+            pair_copies[h, i].wait_recv()
+
     for h, d in enumerate(per_head):
         pair_out[h, 0] = d["A"].astype(BF16)
-        pair_out[h, 1] = jnp.where(half, d["B"], d["C"]).astype(BF16)
-        pair_out[h, 2] = jnp.where(half, d["C"], d["B"]).astype(BF16)
-    for n, part in enumerate((pl.ds(0, 2), pl.ds(2, 1))):
-        for h in range(heads):
-            copy = send(
-                pair_out.at[h, part],
-                pair_in.at[h, part],
-                pair_send.at[h, n],
-                pair_recv.at[h, n],
-                "ctx",
-                me + 1 - 2 * odd,
-            )
-            copy.start()
-            pair_copies.append(copy)
+        pair_out[h, 1] = d["B"].astype(BF16)
+    start_pair(0)
+
+    @pl.when(half)
+    def _():
+        start_pair(1)
+
+    adjoint_part(per_head)
+    for h, d in enumerate(per_head):
+        pair_out[h, 2] = d["C"].astype(BF16)
+    start_pair(2)
+
+    @pl.when(place >= pairs // 2)
+    def _():
+        start_pair(1)
+
     prepared_part(per_head, slope)
     is_odd = odd == 1
 
@@ -357,22 +383,20 @@
         own, other = per_head[h][name], pair_in[h, slot].astype(F32)
         return jnp.where(is_odd, other, own), jnp.where(is_odd, own, other)
 
-    def merge_forward(slot):
+    def merge_forward():
+        wait_pair(1)
         for h in range(heads):
-            (_, a_late), (b_early, b_late) = ordered(h, "A", 0), ordered(h, "B", slot)
+            (_, a_late), (b_early, b_late) = ordered(h, "A", 0), ordered(h, "B", 1)
             merged[h, 1] = nn(b_early, a_late, True) + b_late
 
-    def merge_backward(slot):
+    def merge_backward():
+        wait_pair(2)
         for h in range(heads):
-            (a_early, _), (c_early, c_late) = ordered(h, "A", 0), ordered(h, "C", slot)
+            (a_early, _), (c_early, c_late) = ordered(h, "A", 0), ordered(h, "C", 2)
             merged[h, 2] = nt(c_late, a_early, True) + c_early
 
-    def wait_rest():
-        for copy in pair_copies[heads:]:
-            copy.wait_recv()
-
+    wait_pair(0)
     for h in range(heads):
-        pair_copies[h].wait_recv()
         a_early, a_late = ordered(h, "A", 0)
         merged[h, 0] = nn(a_early, a_late, True)
 
@@ -437,28 +461,24 @@
 
     @pl.when(half)
     def _():
-        merge_forward(1)
+        merge_forward()
         forward()
-        wait_rest()
-        merge_backward(2)
+        merge_backward()
         backward()
 
     @pl.when(place >= pairs // 2)
     def _():
-        merge_backward(1)
+        merge_backward()
         backward()
-        wait_rest()
-        merge_forward(2)
+        merge_forward()
         forward()
 
     states = []
     for h in range(heads):
         start, arriving = chain_in[0, h], chain_in[1, h]
         a_early, a_late = ordered(h, "A", 0)
-        other_b = jnp.where(half, pair_in[h, 1], pair_in[h, 2]).astype(F32)
-        other_c = jnp.where(half, pair_in[h, 2], pair_in[h, 1]).astype(F32)
-        b_early = jnp.where(is_odd, other_b, per_head[h]["B"])
-        c_late = jnp.where(is_odd, per_head[h]["C"], other_c)
+        b_early, _ = ordered(h, "B", 1)
+        _, c_late = ordered(h, "C", 2)
         start_odd = nn(start, a_early, True) + b_early
         arriving_even = nt(arriving, a_late, True) + c_late
         states.append(
@@ -472,7 +492,48 @@
         grads.at[:, 0:8, :], spill, spill_sems.at[0], spill_sems.at[1], "ctx", (me + ctx - 1) % ctx
     )
     spill_copy.start()
-    tap_sums(ext, grads, taps.at[me])
+    width = w.shape[2]
+    edge = count - 16
+    chunks, _, span = total.shape
+
+    def product(c, rows):
+        part = None
+        for m in range(3):
+            term = nt(
+                rounded[rows, m * width : (m + 1) * width], w[m, c * span : (c + 1) * span, :]
+            )
+            part = term if part is None else part + term
+        total[c, rows] = part
+
+    for m in range(3):
+        rounded[:edge, m * width : (m + 1) * width] = raw_part(cw, grads, m, 0, edge)
+    early_chunks = range(min(2, chunks))
+    for c in early_chunks:
+        product(c, slice(0, edge))
+    spill_copy.wait()
+    grads[:, count:, :] = jnp.where(me == ctx - 1, jnp.zeros_like(spill), spill[...])
+    for m in range(3):
+        rounded[edge:, m * width : (m + 1) * width] = raw_part(cw, grads, m, edge, 16)
+    for c in early_chunks:
+        product(c, slice(edge, count))
+    block = count // head_axis
+    sibling = head_me + 1 - 2 * (head_me % 2)
+    far = (head_me + 2) % 4
+
+    def rows_of(c, owner):
+        return total[c, pl.ds(pl.multiple_of(owner * block, 16), block), :]
+
+    near_copies, far_copies = [], []
+
+    def pass_on(c):
+        near_copies[c].wait_recv()
+        far_out[c] = (rows_of(c, far) + near_in[c, block:].astype(F32)).astype(BF16)
+        copy = send(
+            far_out.at[c], far_in.at[c], far_send.at[c], far_recv.at[c], "head", far
+        )
+        copy.start()
+        far_copies.append(copy)
+
     taps_copies = [
         send(
             taps.at[me],
@@ -484,49 +545,8 @@
         )
         for d in range(1, ctx)
     ]
-    for copy in taps_copies:
-        copy.start()
-    width = w.shape[2]
-    edge = count - 16
-    chunks, _, span = total.shape
-
-    def product(c, rows):
-        part = None
-        for m in range(3):
-            term = nt(
-                rounded[rows, m * width : (m + 1) * width], w[m, c * span : (c + 1) * span, :]
-            )
-            part = term if part is None else part + term
-        total[c, rows] = part
-
-    for m in range(3):
-        rounded[:edge, m * width : (m + 1) * width] = raw_part(cw, grads, m, 0, edge)
-    product(0, slice(0, edge))
-    spill_copy.wait()
-    grads[:, count:, :] = jnp.where(me == ctx - 1, jnp.zeros_like(spill), spill[...])
-    for m in range(3):
-        rounded[edge:, m * width : (m + 1) * width] = raw_part(cw, grads, m, edge, 16)
-    product(0, slice(edge, count))
-    block = count // head_axis
-    sibling = head_me + 1 - 2 * (head_me % 2)
-    far = (head_me + 2) % 4
-
-    def rows_of(c, owner):
-        return total[c, pl.ds(pl.multiple_of(owner * block, 16), block), :]
-
-    near_copies, far_copies = [], []
-
-    def pass_on(c):
-        near_copies[c].wait_recv()
-        far_out[c] = (rows_of(c, far) + near_in[c, block:].astype(F32)).astype(BF16)
-        copy = send(
-            far_out.at[c], far_in.at[c], far_send.at[c], far_recv.at[c], "head", far
-        )
-        copy.start()
-        far_copies.append(copy)
-
     for c in range(chunks):
-        if c > 0:
+        if c not in early_chunks:
             product(c, slice(0, count))
         near_out[c, :block] = rows_of(c, sibling).astype(BF16)
         near_out[c, block:] = rows_of(c, (sibling + 2) % 4).astype(BF16)
@@ -535,6 +555,10 @@
         )
         copy.start()
         near_copies.append(copy)
+        if c == early_chunks[-1]:
+            tap_sums(ext, grads, taps.at[me])
+            for copy in taps_copies:
+                copy.start()
         if c > 0:
             pass_on(c - 1)
     pass_on(chunks - 1)
@@ -549,7 +573,7 @@
         far_copies[c].wait_recv()
         result = rows_of(c, head_me) + near_in[c, :block].astype(F32) + far_in[c].astype(F32)
         out[:, c * span : (c + 1) * span] = result.astype(BF16)
-    for copy in near_copies + far_copies + pair_copies:
+    for copy in near_copies + far_copies + list(pair_copies.values()):
         copy.wait_send()
 
     @pl.when(place < pairs - 1)
@@ -612,8 +636,8 @@
             dma((8,)),
             dma((2,)),
             dma((2,)),
-            dma((heads, 2)),
-            dma((heads, 2)),
+            dma((heads, 3)),
+            dma((heads, 3)),
             dma((2, heads)),
             dma((2, heads)),
             dma((ctx - 1,)),

time: 46.6 us -> 44.6 us (0.957)
  Pallas kernels: 45.8 us -> 43.8 us
    pallas_call x1, Pallas kernels: 44.1 us -> 42.2 us  [on_device(): pl.pallas_call(functools.partial(whole_kernel, heads), out_shape=(jax.Sha...]
where the time goes in v6:
time: 44.6 us; the launch traced here: 44.5 us
  Pallas kernels  43.8 us (98%)
  between operations  0.64 us (1%)
    pallas_call x1, Pallas kernels, on_device(): pl.pallas_call(functools.partial(whole_kernel, heads), out_shape=(jax.Sha...  42.2 us
    pallas_call x1, Pallas kernels, on_device(): pl.pallas_call(store_kernel, out_shape=(jax.ShapeDtypeStruct((block, dept...  1.62 us

profile of v6, /device:TPU:0, one launch (start us, length us, event | category | flops | bytes accessed | tf_op | source)
XLA Modules:
  0.0 44.5 jit_solution(14855975522111197983)
XLA Ops:
  0.6 42.2 %shard_map.77 = (bf16[48,2048]{1,0:T(8,128)(2,1)}, f32[3,4,256]{2,1,0:T(4,128)}) custom-call(bf16[192,2048]{1,0:T(8,128)(2,1)} %x_hbm.1, bf16[3,2048,256]{2,1,0:T(8,128)(2,1)} %w_hbm.1, f32[3,4,256]{2,1,0:T(4,128)} %cw_hbm.1, s32[2,192]{1,0:T(2,128)} %gate_hbm.1, s32[2,192]{1,0:T(2,128)} %beta_hbm.1, bf16[192,256]{1,0:T(8,128)(2,1)} %g_hbm.1), custom_call_target="tpu_custom_call" | custom-call | tf_op jit(solution)/shard_map/pallas_call | solution.py:604
  42.8 1.6 %shard_map.78 = (bf16[48,2048]{1,0:T(8,128)(2,1)}, f32[3,4,256]{2,1,0:T(4,128)}) custom-call(bf16[48,2048]{1,0:T(8,128)(2,1)} %get-tuple-element.4.grad, f32[3,4,256]{2,1,0:T(4,128)} %get-tuple-element.5.taps), custom_call_target="tpu_custom_call" | custom-call | tf_op jit(solution)/shard_map/pallas_call | solution.py:654

commit v7 on v6

--- a/solution.py
+++ b/solution.py
@@ -507,7 +507,7 @@
 
     for m in range(3):
         rounded[:edge, m * width : (m + 1) * width] = raw_part(cw, grads, m, 0, edge)
-    early_chunks = range(min(2, chunks))
+    early_chunks = range(min(4, chunks))
     for c in early_chunks:
         product(c, slice(0, edge))
     spill_copy.wait()
@@ -555,7 +555,7 @@
         )
         copy.start()
         near_copies.append(copy)
-        if c == early_chunks[-1]:
+        if c == 1:
             tap_sums(ext, grads, taps.at[me])
             for copy in taps_copies:
                 copy.start()
@@ -597,7 +597,7 @@
     heads = gate_code.shape[0]
     width = heads * DK
     ctx, head_axis = lax.axis_size("ctx"), lax.axis_size("head")
-    chunks = 4
+    chunks = 8
     span = depth // chunks
     block = count // head_axis
     dma = pltpu.SemaphoreType.DMA

time: 44.6 us -> 45.5 us (1.020)
  Pallas kernels: 43.8 us -> 44.7 us
    pallas_call x1, Pallas kernels: 42.2 us -> 43.1 us  [on_device(): pl.pallas_call(functools.partial(whole_kernel, heads), out_shape=(jax.Sha...]
where the time goes in v7:
time: 45.5 us; the launch traced here: 45.4 us
  Pallas kernels  44.7 us (98%)
  between operations  0.64 us (1%)
    pallas_call x1, Pallas kernels, on_device(): pl.pallas_call(functools.partial(whole_kernel, heads), out_shape=(jax.Sha...  43.1 us
    pallas_call x1, Pallas kernels, on_device(): pl.pallas_call(store_kernel, out_shape=(jax.ShapeDtypeStruct((block, dept...  1.62 us

profile of v7, /device:TPU:0, one launch (start us, length us, event | category | flops | bytes accessed | tf_op | source)
XLA Modules:
  0.0 45.4 jit_solution(999792690879702403)
XLA Ops:
  0.6 43.1 %shard_map.77 = (bf16[48,2048]{1,0:T(8,128)(2,1)}, f32[3,4,256]{2,1,0:T(4,128)}) custom-call(bf16[192,2048]{1,0:T(8,128)(2,1)} %x_hbm.1, bf16[3,2048,256]{2,1,0:T(8,128)(2,1)} %w_hbm.1, f32[3,4,256]{2,1,0:T(4,128)} %cw_hbm.1, s32[2,192]{1,0:T(2,128)} %gate_hbm.1, s32[2,192]{1,0:T(2,128)} %beta_hbm.1, bf16[192,256]{1,0:T(8,128)(2,1)} %g_hbm.1), custom_call_target="tpu_custom_call" | custom-call | tf_op jit(solution)/shard_map/pallas_call | solution.py:604
  43.7 1.6 %shard_map.78 = (bf16[48,2048]{1,0:T(8,128)(2,1)}, f32[3,4,256]{2,1,0:T(4,128)}) custom-call(bf16[48,2048]{1,0:T(8,128)(2,1)} %get-tuple-element.4.grad, f32[3,4,256]{2,1,0:T(4,128)} %get-tuple-element.5.taps), custom_call_target="tpu_custom_call" | custom-call | tf_op jit(solution)/shard_map/pallas_call | solution.py:654
